TPU v7x, 256 devices: a whole 4x4x8 slice. The times are simulated.
256 devices in a mesh: group: 8 (over y, core), tile: 32 (over x, z).
Axes of the slice: x: 4, y: 4, z: 8, core: 2. Of those that a mesh axis runs over, the one named last changes fastest.
Arguments:
- raw_pulses: bfloat16 [512, 4, 2, 16384], P(('group', 'tile')), may hold values from -6 to 6
- chirp_taps: float32 [2, 1024], replicated, may hold values from -0.125 to 0.125
- phase_error: float32 [512], P(('group', 'tile')), may hold values from -3.140625 to 3.140625
- illumination: int32 [256, 256, 2], P(('group', 'tile')), may hold values from 0 to 2, as said below
- swath_start: int32 [256, 256, 2], P(('group', 'tile')), may hold values from 0 to 124
- range_bins: int32 [256, 8, 256], P(('group', 'tile')), may hold values from 0 to 511
- cross_range: float32 [256, 256], P(('group', 'tile')), may hold values from -2 to 2
Outputs:
- image_tile: float32 [256, 4, 2, 256], P(('group', 'tile'))
- phase_grad: float32 [512], P(('group', 'tile'))
Inputs may be any that keep to these rules, and one draw needn't show every extreme that they name: `illumination`: the local pulse of block d sent in slot c to tile e; 2 marks an empty slot; each tile has its own share of filled slots.
All inputs are finite; a program needn't handle non-finite values.
Results may differ from a plain program's by a relative error of at most 0.008.
Values may be sent and summed in bfloat16 or wider, within the bound.
No kernel may reach another device: no remote copies, remote signals or barrier semaphores. Data moves between devices by JAX's collectives and lax.ppermute only.
A program may use at most 128 MiB of HBM per device.

v0:
```python
import functools
import math

import jax
import jax.numpy as jnp
from jax import lax
from jax.experimental import pallas as pl
from jax.experimental.pallas import tpu as pltpu
from jax.sharding import Mesh, PartitionSpec as P

TAPS = 1024
RBINS = 16384
POLS = 4
SWATH = 512
PIX = 256
TILES = 256
GROUPS = 8
PLANE = 32
ROWS = 2 * POLS
BLOCK = 256
BLOCKS = RBINS // BLOCK
NOTE_ROWS = 16
SPAN = TAPS + BLOCK
IMAGE_SCALE = 1.0 / math.sqrt(TILES * 2)
GRAD_SCALE = IMAGE_SCALE / math.sqrt(PIX * POLS)
VMEM_LIMIT = 48 * 1024 * 1024
BLOCK_ORDER = ((0, 0), (0, 1), (1, 0), (1, 1), (3, 0), (3, 1), (2, 0), (2, 1))
SMEM = pl.BlockSpec(memory_space=pltpu.SMEM)
VMEM = pl.BlockSpec(memory_space=pltpu.VMEM)
PARAMS = pltpu.CompilerParams(vmem_limit_bytes=VMEM_LIMIT)


def row_sign(shape, axis):
    return jnp.where(lax.broadcasted_iota(jnp.int32, shape, axis) < POLS, -1.0, 1.0)


def three_parts(x):
    first = x.astype(jnp.bfloat16).astype(jnp.float32)
    second = (x - first).astype(jnp.bfloat16).astype(jnp.float32)
    return [first, second, x - first - second]


def compress_kernel(
    raw_ref, taps_ref, error_ref, chosen_ref, start_ref, bins_ref, cross_ref, out_ref, known_ref, left_ref, odd_ref
):
    known = [bins_ref[...].astype(jnp.float32) - 256.0] + three_parts(cross_ref[...])
    known.append(jnp.zeros((5, PIX), jnp.float32))
    known = jnp.concatenate(known, axis=0).astype(jnp.bfloat16)
    for at in range(PLANE):
        known_ref[at] = known

    taps = taps_ref[...].astype(jnp.bfloat16).astype(jnp.float32)
    wide = []
    for part in range(2):
        rows = jnp.broadcast_to(taps[part : part + 1], (BLOCK, SPAN))
        wide.append(pltpu.roll(rows, 0, 1, stride=1, stride_axis=0))
    matrices = []
    for j in range(SPAN // BLOCK):
        lanes = slice(j * BLOCK, (j + 1) * BLOCK)
        matrices.append(jnp.concatenate([rows[:, lanes].T for rows in wide], axis=0).astype(jnp.bfloat16))

    total = BLOCKS * ROWS
    for pulse in range(2):
        first = raw_ref[pulse * total : (pulse + 1) * total].astype(jnp.float32)
        second = pltpu.roll(first.reshape(BLOCKS, ROWS, BLOCK), POLS, 1)
        second = (second * -row_sign((BLOCKS, ROWS, BLOCK), 1)).reshape(total, BLOCK)
        both = jnp.concatenate([first, second], axis=1)
        edge = jnp.zeros((SPAN // BLOCK * ROWS, 2 * BLOCK), jnp.float32)
        left_ref[...] = jnp.concatenate([both, edge[ROWS:]], axis=0).astype(jnp.bfloat16)
        odd_ref[...] = jnp.concatenate([both[ROWS:], edge], axis=0).astype(jnp.bfloat16)
        sums = None
        for j in range(SPAN // BLOCK):
            source = odd_ref if j % 2 else left_ref
            at = j // 2 * 2 * ROWS
            part = jnp.dot(source[at : at + total], matrices[j], preferred_element_type=jnp.float32)
            sums = part if sums is None else sums + part
        sums = sums.reshape(BLOCKS, ROWS, BLOCK)
        out_ref[pulse * BLOCKS : (pulse + 1) * BLOCKS] = jnp.concatenate(
            [sums[:, :, :128], sums[:, :, 128:]], axis=1
        ).astype(jnp.bfloat16)

    rows = [chosen_ref[...].astype(jnp.float32), start_ref[...].astype(jnp.float32)]
    for pulse in range(2):
        rows += three_parts(jnp.full((1, PIX), error_ref[pulse], jnp.float32))
    rows.append(jnp.zeros((NOTE_ROWS - 10, PIX), jnp.float32))
    rows = jnp.concatenate(rows, axis=0).astype(jnp.bfloat16)
    out_ref[2 * BLOCKS] = rows[:, :128]
    out_ref[2 * BLOCKS + 1] = rows[:, 128:]


def compress(raw, taps, phase_error, chosen, start, bins, cross):
    return pl.pallas_call(
        compress_kernel,
        out_shape=(
            jax.ShapeDtypeStruct((2 * BLOCKS + 2, 2 * ROWS, 128), jnp.bfloat16),
            jax.ShapeDtypeStruct((PLANE, 16, PIX), jnp.bfloat16),
        ),
        in_specs=[VMEM, VMEM, SMEM, VMEM, VMEM, VMEM, VMEM],
        out_specs=(VMEM, VMEM),
        scratch_shapes=[
            pltpu.VMEM((BLOCKS * ROWS + 4 * ROWS, 2 * BLOCK), jnp.bfloat16),
            pltpu.VMEM((BLOCKS * ROWS + 4 * ROWS, 2 * BLOCK), jnp.bfloat16),
        ],
        compiler_params=PARAMS,
        name="compress",
    )(raw, taps, phase_error, chosen, start, bins, cross)


def shift_kernel(count, *refs):
    out_ref = refs[count]
    for dev in range(count):
        out_ref[dev, 0] = refs[dev][: 2 * BLOCKS]
        rows = refs[dev][: 2 * BLOCKS].astype(jnp.float32)
        later = jnp.concatenate([rows[1:, :ROWS], rows[:1, :ROWS]], axis=0)
        out_ref[dev, 1] = jnp.concatenate([rows[:, ROWS:], later], axis=1).astype(jnp.bfloat16)


def shifted(pulses):
    count = len(pulses)
    return pl.pallas_call(
        functools.partial(shift_kernel, count),
        out_shape=jax.ShapeDtypeStruct((count, 2, 2 * BLOCKS, 2 * ROWS, 128), jnp.bfloat16),
        in_specs=[VMEM] * count,
        out_specs=VMEM,
        compiler_params=PARAMS,
        name="shift",
    )(*pulses).reshape(count * 4 * BLOCKS, 2 * ROWS, 128)


def kappa_phase(bins):
    turned = 31.0 * bins
    left = turned - 97.0 * jnp.floor((turned + 0.5) * (1.0 / 97.0))
    return left * (2.0 * math.pi / 97.0)


def lists_kernel(group_ref, *refs):
    note_refs, whole_ref, turn_ref = refs[:GROUPS], refs[GROUPS], refs[GROUPS + 1]
    notes = [jnp.concatenate([ref[0], ref[1]], axis=1).astype(jnp.float32) for ref in note_refs]
    rows, chosen, cosines, sines = [], [], [], []
    for slot in range(2):
        pulse = jnp.concatenate([note[slot : slot + 1] for note in notes], axis=0)
        start = jnp.concatenate([note[2 + slot : 3 + slot] for note in notes], axis=0)
        errors = [
            jnp.concatenate([note[at : at + 1] + note[at + 1 : at + 2] + note[at + 2 : at + 3] for note in notes], axis=0)
            for at in (4, 7)
        ]
        rotation = kappa_phase(128.0 * start) - jnp.where(pulse < 0.5, errors[0], errors[1])
        filled = pulse < 1.5
        pair = jnp.floor(0.5 * start)
        rows.append((2.0 * (start - 2.0 * pair) + jnp.minimum(pulse, 1.0)) * BLOCKS + pair)
        chosen.append(pulse)
        cosines.append(jnp.where(filled, jnp.cos(rotation), 0.0))
        sines.append(jnp.where(filled, jnp.sin(rotation), 0.0))
    shift = (TILES - group_ref[0] * PLANE) % TILES
    for parts, ref in ((rows + chosen, whole_ref), (cosines + sines, turn_ref)):
        parts = jnp.concatenate(parts + [jnp.zeros((128 - 4 * GROUPS, TILES), jnp.float32)], axis=0)
        parts = pltpu.roll(parts, shift, 1)[:, :128]
        ref[...] = parts.T[:PLANE].astype(ref.dtype)


def lists(group, pulses):
    note = pl.BlockSpec((2, NOTE_ROWS, 128), lambda i: (BLOCKS, 0, 0))
    out = pl.BlockSpec((PLANE, 128), lambda i: (0, 0))
    return pl.pallas_call(
        lists_kernel,
        grid=(1,),
        out_shape=(
            jax.ShapeDtypeStruct((PLANE, 128), jnp.int32),
            jax.ShapeDtypeStruct((PLANE, 128), jnp.float32),
        ),
        in_specs=[SMEM] + [note] * GROUPS,
        out_specs=(out, out),
        compiler_params=PARAMS,
        name="lists",
    )(group, *pulses)


def phase_kernel(group_ref, rate_ref, known_ref, bins_ref, phase_ref):
    cross = known_ref[8].astype(jnp.float32) + known_ref[9].astype(jnp.float32)
    cross = cross + known_ref[10].astype(jnp.float32)
    for dev in range(GROUPS):
        bins = known_ref[group_ref[dev]].astype(jnp.float32) + 256.0
        angle = kappa_phase(bins) + rate_ref[dev] * cross
        phase_ref[dev, 0] = jnp.cos(angle)
        phase_ref[dev, 1] = jnp.sin(angle)
        bins_ref[dev] = bins.astype(jnp.int32)


def phases(groups, rates, known):
    return pl.pallas_call(
        phase_kernel,
        out_shape=(
            jax.ShapeDtypeStruct((GROUPS, PLANE, PIX), jnp.int32),
            jax.ShapeDtypeStruct((GROUPS, 2, PLANE, PIX), jnp.float32),
        ),
        in_specs=[SMEM, SMEM, VMEM],
        out_specs=(VMEM, VMEM),
        compiler_params=PARAMS,
        name="phases",
    )(groups, rates, known)


def pick_lanes(rows, lanes):
    dims = lax.GatherDimensionNumbers(
        offset_dims=(),
        collapsed_slice_dims=(1,),
        start_index_map=(1,),
        operand_batching_dims=(0,),
        start_indices_batching_dims=(0,),
    )
    return lax.gather(rows, lanes[..., None], dims, slice_sizes=(1, 1), mode="promise_in_bounds")


def image_kernel(whole_ref, turn_ref, bins_ref, phase_ref, comp_a, comp_b, comp_c, part_ref, kept_ref, sum_ref):
    sign = row_sign((ROWS, 128), 0)
    homes = [(comp_a, 0), (comp_a, 1), (comp_b, 0), (comp_b, 1), (comp_b, 2), (comp_b, 3), (comp_c, 0), (comp_c, 1)]

    def step(tile, carry):
        total = [None, None]
        for dev in range(GROUPS):
            comp_ref, home = homes[dev]
            bins = bins_ref[dev, pl.ds(tile, 1), :]
            cos_row = phase_ref[dev, 0, pl.ds(tile, 1), :]
            sin_row = phase_ref[dev, 1, pl.ds(tile, 1), :]
            sources = []
            for slot in range(2):
                base = whole_ref[tile, slot * GROUPS + dev] + home * 4 * BLOCKS
                sources.append((comp_ref[base], comp_ref[base + 1]))
            cos_rot = [turn_ref[tile, slot * GROUPS + dev] for slot in range(2)]
            sin_rot = [turn_ref[tile, (2 + slot) * GROUPS + dev] * sign for slot in range(2)]
            for half in range(2):
                lanes = slice(half * 128, (half + 1) * 128)
                where = jnp.broadcast_to(bins[:, lanes], (ROWS, 128))
                lane = where & 127
                odd = (where & 128) != 0
                high = (where & 256) != 0
                lane = jnp.concatenate([lane, lane], axis=0).astype(jnp.int16)
                turned = []
                for slot in range(2):
                    low, top = [pick_lanes(source, lane).astype(jnp.float32) for source in sources[slot]]
                    value = jnp.where(
                        high, jnp.where(odd, top[ROWS:], top[:ROWS]), jnp.where(odd, low[ROWS:], low[:ROWS])
                    )
                    value = cos_rot[slot] * value + sin_rot[slot] * pltpu.roll(value, POLS, 0)
                    turned.append(value.astype(jnp.bfloat16))
                kept_ref[tile, dev, :, lanes] = jnp.concatenate(turned, axis=0)
                summed = turned[0].astype(jnp.float32) + turned[1].astype(jnp.float32)
                term = jnp.broadcast_to(cos_row[:, lanes], (ROWS, 128)) * summed + jnp.broadcast_to(
                    sin_row[:, lanes], (ROWS, 128)
                ) * (sign * pltpu.roll(summed, POLS, 0))
                total[half] = term if total[half] is None else total[half] + term
        sum_ref[tile] = jnp.concatenate(total, axis=1)
        return carry

    lax.fori_loop(0, PLANE, step, 0)
    part_ref[...] = sum_ref[...].reshape(PLANE * ROWS, PIX).astype(jnp.bfloat16)


def image_parts(whole, turn, bins, phase, comps):
    return pl.pallas_call(
        image_kernel,
        out_shape=(
            jax.ShapeDtypeStruct((PLANE * ROWS, PIX), jnp.bfloat16),
            jax.ShapeDtypeStruct((PLANE, GROUPS, 2 * ROWS, PIX), jnp.bfloat16),
        ),
        in_specs=[SMEM, SMEM] + [VMEM] * 5,
        out_specs=(VMEM, VMEM),
        scratch_shapes=[pltpu.VMEM((PLANE, ROWS, PIX), jnp.float32)],
        compiler_params=PARAMS,
        name="image",
    )(whole, turn, bins, phase, *comps)


def total_kernel(parts_ref, tile_ref, copies_ref):
    image = IMAGE_SCALE * jnp.sum(parts_ref[...].astype(jnp.float32), axis=0)
    for row in range(ROWS):
        tile_ref[row % POLS, row // POLS, :] = image[row]
    for at in range(PLANE):
        copies_ref[at] = image


def total_image(parts):
    return pl.pallas_call(
        total_kernel,
        out_shape=(
            jax.ShapeDtypeStruct((POLS, 2, PIX), jnp.float32),
            jax.ShapeDtypeStruct((PLANE, ROWS, PIX), jnp.float32),
        ),
        in_specs=[VMEM],
        out_specs=(VMEM, VMEM),
        compiler_params=PARAMS,
        name="total",
    )(parts)


def grad_kernel(group_ref, whole_ref, image_ref, kept_ref, phase_ref, out_ref):
    sign = row_sign((ROWS, 128), 0)

    def step(tile, sums):
        sums = list(sums)
        firsts, seconds = [], []
        for half in range(2):
            image = image_ref[tile, :, half * 128 : (half + 1) * 128]
            other = pltpu.roll(image, POLS, 0)
            size = 4.0 * (image * image + other * other)
            firsts.append(size * image)
            seconds.append((size * other) * sign)
        for dev in range(GROUPS):
            cos_row = phase_ref[dev, 0, pl.ds(tile, 1), :]
            sin_row = phase_ref[dev, 1, pl.ds(tile, 1), :]
            weights = []
            for half in range(2):
                lanes = slice(half * 128, (half + 1) * 128)
                weights.append(
                    firsts[half] * jnp.broadcast_to(sin_row[:, lanes], (ROWS, 128))
                    + seconds[half] * jnp.broadcast_to(cos_row[:, lanes], (ROWS, 128))
                )
            kept = kept_ref[tile, dev].astype(jnp.float32)
            for slot in range(2):
                value = kept[slot * ROWS : (slot + 1) * ROWS]
                term = weights[0] * value[:, :128] + weights[1] * value[:, 128:]
                pulse = whole_ref[tile, (2 + slot) * GROUPS + dev]
                for which in range(2):
                    at = dev * 2 + which
                    sums[at] = sums[at] + jnp.where(pulse == which, 1.0, 0.0) * term
        return tuple(sums)

    zero = jnp.zeros((ROWS, 128), jnp.float32)
    sums = lax.fori_loop(0, PLANE, step, (zero,) * (2 * GROUPS))
    lane = lax.broadcasted_iota(jnp.int32, (ROWS, 128), 1)
    for dev in range(GROUPS):
        pair = [jnp.sum(sums[dev * 2 + which], keepdims=True) * GRAD_SCALE for which in range(2)]
        out_ref[group_ref[dev]] = jnp.where(lane == 0, pair[0], pair[1])


def grad_parts(groups, whole, image, kept, phase):
    return pl.pallas_call(
        grad_kernel,
        out_shape=jax.ShapeDtypeStruct((GROUPS, ROWS, 128), jnp.float32),
        in_specs=[SMEM, SMEM] + [VMEM] * 3,
        out_specs=VMEM,
        compiler_params=PARAMS,
        name="grad",
    )(groups, whole, image, kept, phase)


def body(raw_pulses, chirp_taps, phase_error, illumination, swath_start, range_bins, cross_range):
    core = lax.axis_index("core")
    at_y = lax.axis_index("y")
    at_plane = lax.axis_index(("x", "z"))
    groups = jnp.stack([2 * ((at_y + 4 - back) % 4) + (core + other) % 2 for back, other in BLOCK_ORDER])
    rates = math.pi * (2 * (groups * PLANE + at_plane) + 1 - TILES).astype(jnp.float32) / TILES

    raw = raw_pulses.reshape(2, POLS, 2, BLOCKS, BLOCK).transpose(0, 3, 2, 1, 4)
    own, known = compress(
        raw.reshape(2 * BLOCKS * ROWS, BLOCK),
        jnp.pad(chirp_taps, ((0, 0), (0, SPAN - TAPS))),
        phase_error,
        illumination[0].T,
        swath_start[0].T,
        range_bins[0],
        cross_range,
    )
    line = {0: own}
    for back in (1, 3, 2):
        line[back] = lax.ppermute(own, "y", [(at, (at + back) % 4) for at in range(4)])
    known = lax.all_to_all(known, ("x", "z"), 0, 0, tiled=True)
    line[1], line[3], line[2], known = lax.optimization_barrier((line[1], line[3], line[2], known))
    pulses = []
    for back in (0, 1, 3, 2):
        pulses += [line[back], lax.ppermute(line[back], "core", [(0, 1), (1, 0)])]

    bins, phase = phases(groups, rates, known.transpose(1, 0, 2))
    comps = [shifted(pulses[:2]), shifted(pulses[2:6]), shifted(pulses[6:])]
    whole, turn = lists(groups[:1], pulses)

    parts, kept = image_parts(whole, turn, bins, phase, comps)
    parts = lax.all_to_all(parts.reshape(PLANE, ROWS, PIX), ("x", "z"), 0, 0, tiled=True)
    image_tile, copies = total_image(parts)
    images = lax.all_to_all(copies, ("x", "z"), 0, 0, tiled=True)
    grads = grad_parts(groups, whole, images, kept, phase)
    grads = lax.all_to_all(grads, ("y", "core"), 0, 0, tiled=True)
    return (image_tile[None], jnp.sum(grads[:, 0, :2], axis=0))


def solution(mesh):
    fine = Mesh(mesh.devices.reshape(4, 2, 4, 8), ("y", "core", "x", "z"))
    every = ("y", "core", "x", "z")
    return jax.shard_map(
        body,
        mesh=fine,
        in_specs=(
            P(every, None, None, None),
            P(),
            P(every),
            P(every, None, None),
            P(every, None, None),
            P(every, None, None),
            P(every, None),
        ),
        out_specs=(P(every, None, None, None), P(every)),
        check_vma=False,
    )
```

profile of v0, /device:TPU:1, one launch (start us, length us, event | category | flops | bytes accessed | tf_op | source)
XLA Modules:
  0.0 102.9 jit_solution(4978545506012373142)
XLA Ops:
  0.6 0.0 copy-start.6
  0.6 0.0 copy-start.4
  0.7 0.0 copy-start.1
  0.7 0.0 copy-start.3
  0.7 0.0 copy-start.2
  0.7 0.0 copy-start.5
  0.7 1.4 %reshape.22 = bf16[2,4,2,64,256]{4,3,2,1,0:T(8,128)(2,1)S(1)} reshape(bf16[2,4,2,16384]{3,2,1,0:T(2,128)(2,1)} %param.7) | data formatting | bytes 1048576 | tf_op jit(solution)/shard_map/reshape | solution.py:354
  2.1 0.4 copy.15
  2.5 0.1 reshape.23.raw_ref
  2.6 0.0 copy-done.6
  2.7 0.0 copy-done.4
  2.7 0.0 copy-done.1
  2.7 0.0 copy-done.3
  2.7 0.0 copy-done.2
  2.7 0.0 copy-done.5
  2.7 2.9 %compress.1 = (bf16[130,16,128]{2,1,0:T(8,128)(2,1)S(1)}, bf16[32,16,256]{2,1,0:T(8,128)(2,1)}) custom-call(bf16[1024,256]{1,0:T(8,128)(2,1)S(1)} %reshape.23.raw_ref, f32[2,1280]{1,0:T(2,128)S(1)} %pad.4.taps_ref, f32[2]{0:T(128)S(1)} %copy-done.5, s32[2,256]{1,0:T(2,128)S(1)} %bitcast.31, s32[2,256]{1,0:T(2,128)S(1)} %bitcast.32, s32[8,256]{1,0:T(8,128)S(1)} %bitcast.30, ...), custom_call_target="tpu_custom_call" | custom-call | tf_op jit(solution)/shard_map/compress/pallas_call | solution.py:92
  5.6 3.7 %collective-permute-start.3 = (bf16[130,16,128]{2,1,0:T(8,128)(2,1)S(1)}, bf16[130,16,128]{2,1,0:T(8,128)(2,1)S(1)}, u32[]{:S(2)}, u32[]{:S(2)}) collective-permute-start(bf16[130,16,128]{2,1,0:T(8,128)(2,1)S(1)} %get-tuple-element.16.refs_0_), channel_id=1, source_target_pairs={{0,128},{64,192},{128,0},{192,64},{1,129},{65,193},{129,1},{193,65... | collective-permute-start | bytes 1597448 | tf_op jit(solution)/shard_map/ppermute | solution.py:366
  9.3 0.8 collective-permute-start.2
  10.1 0.7 collective-permute-start.1
  10.8 11.0 %all-to-all-start = ((bf16[32,16,256]{2,1,0:T(8,128)(2,1)}), bf16[32,16,256]{2,1,0:T(8,128)(2,1)S(1)}, u32[]{:S(2)}, u32[]{:S(2)}) async-start(bf16[32,16,256]{2,1,0:T(8,128)(2,1)} %get-tuple-element.17), calls=%async_computation | async-start | bytes 524288 | tf_op jit(solution)/shard_map/all_to_all | solution.py:367
  21.8 1.9 %collective-permute-start = (bf16[130,16,128]{2,1,0:T(8,128)(2,1)S(1)}, bf16[130,16,128]{2,1,0:T(8,128)(2,1)}, u32[]{:S(2)}, u32[]{:S(2)}) collective-permute-start(bf16[130,16,128]{2,1,0:T(8,128)(2,1)S(1)} %get-tuple-element.16.refs_0_), channel_id=1, source_target_pairs={{0,32},{32,0},{1,33},{33,1},{2,34},{34,2},{3,35},{35,3},{4,36},{36... | collective-permute-start | bytes 1597448 | tf_op jit(solution)/shard_map/ppermute | solution.py:371
  23.7 7.8 %all-to-all-done = bf16[32,16,256]{2,1,0:T(8,128)(2,1)S(1)} async-done(((bf16[32,16,256]{2,1,0:T(8,128)(2,1)}), bf16[32,16,256]{2,1,0:T(8,128)(2,1)S(1)}, u32[]{:S(2)}, u32[]{:S(2)}) %all-to-all-start) | async-done | bytes 262176 | tf_op jit(solution)/shard_map/all_to_all | solution.py:367
  31.5 0.0 collective-permute-done.3.refs_6_.refs_0_
  31.5 1.2 %collective-permute-done.2.refs_4_.refs_2_ = bf16[130,16,128]{2,1,0:T(8,128)(2,1)S(1)} collective-permute-done((bf16[130,16,128]{2,1,0:T(8,128)(2,1)S(1)}, bf16[130,16,128]{2,1,0:T(8,128)(2,1)S(1)}, u32[]{:S(2)}, u32[]{:S(2)}) %collective-permute-start.2) | collective-permute-done | bytes 532512 | tf_op jit(solution)/shard_map/ppermute | solution.py:366
  32.7 0.6 collective-permute-done.1.refs_2_.refs_0_
  33.3 1.9 %collective-permute-start.6 = (bf16[130,16,128]{2,1,0:T(8,128)(2,1)S(1)}, bf16[130,16,128]{2,1,0:T(8,128)(2,1)}, u32[]{:S(2)}, u32[]{:S(2)}) collective-permute-start(bf16[130,16,128]{2,1,0:T(8,128)(2,1)S(1)} %collective-permute-done.3.refs_6_.refs_0_), channel_id=1, source_target_pairs={{0,32},{32,0},{1,33},{33,1},{2,34},{34,2},{3,35},{35,3},{4,36},{36... | collective-permute-start | bytes 1597448 | tf_op jit(solution)/shard_map/ppermute | solution.py:371
  35.2 0.1 collective-permute-start.4
  35.3 0.4 collective-permute-start.5
  35.7 0.1 stack.35.group_ref
  35.8 0.1 copy.16
  35.9 1.6 %phases.1 = (s32[8,32,256]{2,1,0:T(8,128)S(1)}, f32[8,2,32,256]{3,2,1,0:T(8,128)S(1)}) custom-call(s32[8]{0:T(128)S(1)} %stack.35.group_ref, f32[8]{0:T(128)S(1)} %convert_multiply_fusion.rate_ref, bf16[16,32,256]{2,1,0:T(8,128)(2,1)S(1)} %bitcast.28), custom_call_target="tpu_custom_call" | custom-call | tf_op jit(solution)/shard_map/phases/pallas_call | solution.py:190
  37.5 0.0 collective-permute-done.refs_1_
  37.5 1.3 %shift.3 = bf16[2,2,128,16,128]{4,3,2,1,0:T(8,128)(2,1)S(1)} custom-call(bf16[130,16,128]{2,1,0:T(8,128)(2,1)S(1)} %get-tuple-element.16.refs_0_, bf16[130,16,128]{2,1,0:T(8,128)(2,1)} %collective-permute-done.refs_1_), custom_call_target="tpu_custom_call" | custom-call | tf_op jit(solution)/shard_map/shift/pallas_call | solution.py:120
  38.8 0.0 collective-permute-done.6.refs_7_.refs_1_
  38.8 1.3 %shift.5 = bf16[2,2,128,16,128]{4,3,2,1,0:T(8,128)(2,1)S(1)} custom-call(bf16[130,16,128]{2,1,0:T(8,128)(2,1)S(1)} %collective-permute-done.3.refs_6_.refs_0_, bf16[130,16,128]{2,1,0:T(8,128)(2,1)} %collective-permute-done.6.refs_7_.refs_1_), custom_call_target="tpu_custom_call" | custom-call | tf_op jit(solution)/shard_map/shift/pallas_call | solution.py:120
  40.1 0.0 copy-start
  40.1 1.4 %copy-done = bf16[2,2,128,16,128]{4,3,2,1,0:T(8,128)(2,1)} copy-done((bf16[2,2,128,16,128]{4,3,2,1,0:T(8,128)(2,1)}, bf16[2,2,128,16,128]{4,3,2,1,0:T(8,128)(2,1)S(1)}, u32[]{:S(2)}) %copy-start) | copy-done | bytes 2097176
  41.5 0.0 collective-permute-done.4.refs_3_.refs_1_
  41.5 0.0 collective-permute-done.5.refs_5_.refs_3_
  41.5 1.0 lists.1
  42.5 2.5 %shift.4 = bf16[4,2,128,16,128]{4,3,2,1,0:T(8,128)(2,1)} custom-call(bf16[130,16,128]{2,1,0:T(8,128)(2,1)S(1)} %collective-permute-done.1.refs_2_.refs_0_, bf16[130,16,128]{2,1,0:T(8,128)(2,1)S(1)} %collective-permute-done.4.refs_3_.refs_1_, bf16[130,16,128]{2,1,0:T(8,128)(2,1)S(1)} %collective-permute-done.2.refs_4_.refs_2_, ...), custom_call_target="tpu_custom_call" | custom-call | tf_op jit(solution)/shard_map/shift/pallas_call | solution.py:120
  44.9 9.2 %image.1 = (bf16[256,256]{1,0:T(8,128)(2,1)S(1)}, bf16[32,8,16,256]{3,2,1,0:T(8,128)(2,1)S(1)}) custom-call(s32[32,128]{1,0:T(8,128)S(1)} %get-tuple-element.21.whole_ref, f32[32,128]{1,0:T(8,128)S(1)} %get-tuple-element.22.turn_ref, s32[8,32,256]{2,1,0:T(8,128)S(1)} %get-tuple-element.24.bins_ref, f32[8,2,32,256]{3,2,1,0:T(8,128)S(1)} %get-tuple-element.25.phase_ref, ...), custom_call_target="tpu_custom_call" | custom-call | tf_op jit(solution)/shard_map/image/pallas_call | solution.py:260
  54.2 19.0 %all_to_all.20.parts_ref = bf16[32,8,256]{2,1,0:T(8,128)(2,1)S(1)} all-to-all(bf16[32,8,256]{2,1,0:T(8,128)(2,1)S(1)} %bitcast.29), channel_id=1, replica_groups=mesh['y'=4,'core'=2,'x'=4,'z'=8] {'x','z'}, dimensions={0} | all-to-all | bytes 262144 | tf_op jit(solution)/shard_map/all_to_all | solution.py:378
  73.2 0.7 total.1
  73.8 14.0 %all_to_all.21.image_ref = f32[32,8,256]{2,1,0:T(8,128)S(1)} all-to-all(f32[32,8,256]{2,1,0:T(8,128)S(1)} %get-tuple-element.28), channel_id=1, replica_groups=mesh['y'=4,'core'=2,'x'=4,'z'=8] {'x','z'}, dimensions={0} | all-to-all | bytes 524288 | tf_op jit(solution)/shard_map/all_to_all | solution.py:380
  87.8 2.3 %grad.1 = f32[8,8,128]{2,1,0:T(8,128)S(1)} custom-call(s32[8]{0:T(128)S(1)} %stack.35.group_ref, s32[32,128]{1,0:T(8,128)S(1)} %get-tuple-element.21.whole_ref, f32[32,8,256]{2,1,0:T(8,128)S(1)} %all_to_all.21.image_ref, bf16[32,8,16,256]{3,2,1,0:T(8,128)(2,1)S(1)} %get-tuple-element.29.kept_ref, f32[8,2,32,256]{3,2,1,0:T(8,128)S(1)} %get-tuple-element.25.phase_ref), custom_call_target="tpu_custom_call" | custom-call | tf_op jit(solution)/shard_map/grad/pallas_call | solution.py:337
  90.1 12.2 %all_to_all.22 = f32[8,8,128]{2,1,0:T(8,128)S(1)} all-to-all(f32[8,8,128]{2,1,0:T(8,128)S(1)} %grad.1), channel_id=1, replica_groups=mesh['y'=4,'core'=2,'x'=4,'z'=8] {'y','core'}, dimensions={0} | all-to-all | bytes 65536 | tf_op jit(solution)/shard_map/all_to_all | solution.py:382
  102.3 0.5 slice_reduce_fusion
  (2 shorter events, 0.0 us)
Async XLA Ops:
  0.6 2.0 %copy-start.6 = (f32[2,1024]{1,0:T(2,128)S(1)}, f32[2,1024]{1,0:T(2,128)}, u32[]{:S(2)}) copy-start(f32[2,1024]{1,0:T(2,128)} %param.8) | copy-start | bytes 24580
  0.6 2.0 %copy-start.4 = (f32[1,256]{1,0:T(1,128)S(1)}, f32[1,256]{1,0:T(1,128)}, u32[]{:S(2)}) copy-start(f32[1,256]{1,0:T(1,128)} %cross_ref.1) | copy-start | bytes 3076
  0.7 2.0 %copy-start.1 = (s32[1,8,256]{2,1,0:T(8,128)S(1)}, s32[1,8,256]{2,1,0:T(8,128)}, u32[]{:S(2)}) copy-start(s32[1,8,256]{2,1,0:T(8,128)} %param.12) | copy-start | bytes 24580
  0.7 2.0 %copy-start.3 = (s32[1,256,2]{1,2,0:T(2,128)S(1)}, s32[1,256,2]{1,2,0:T(2,128)}, u32[]{:S(2)}) copy-start(s32[1,256,2]{1,2,0:T(2,128)} %param.11) | copy-start | bytes 6148
  0.7 2.0 %copy-start.2 = (s32[1,256,2]{1,2,0:T(2,128)S(1)}, s32[1,256,2]{1,2,0:T(2,128)}, u32[]{:S(2)}) copy-start(s32[1,256,2]{1,2,0:T(2,128)} %param.10) | copy-start | bytes 6148
  0.7 2.0 %copy-start.5 = (f32[2]{0:T(128)S(1)}, f32[2]{0:T(128)}, u32[]{:S(2)}) copy-start(f32[2]{0:T(128)} %error_ref.1) | copy-start | bytes 28
  5.6 25.9 %collective-permute-start.3 = (bf16[130,16,128]{2,1,0:T(8,128)(2,1)S(1)}, bf16[130,16,128]{2,1,0:T(8,128)(2,1)S(1)}, u32[]{:S(2)}, u32[]{:S(2)}) collective-permute-start(bf16[130,16,128]{2,1,0:T(8,128)(2,1)S(1)} %get-tuple-element.16.refs_0_), channel_id=1, source_target_pairs={{0,128},{64,192},{128,0},{192,64},{1,129},{65,193},{129,1},{193,65... | collective-permute-start | bytes 1597448 | tf_op jit(solution)/shard_map/ppermute | solution.py:366
  9.3 23.4 %collective-permute-start.2 = (bf16[130,16,128]{2,1,0:T(8,128)(2,1)S(1)}, bf16[130,16,128]{2,1,0:T(8,128)(2,1)S(1)}, u32[]{:S(2)}, u32[]{:S(2)}) collective-permute-start(bf16[130,16,128]{2,1,0:T(8,128)(2,1)S(1)} %get-tuple-element.16.refs_0_), channel_id=1, source_target_pairs={{0,192},{64,0},{128,64},{192,128},{1,193},{65,1},{129,65},{193,129... | collective-permute-start | bytes 1597448 | tf_op jit(solution)/shard_map/ppermute | solution.py:366
  10.1 23.2 %collective-permute-start.1 = (bf16[130,16,128]{2,1,0:T(8,128)(2,1)S(1)}, bf16[130,16,128]{2,1,0:T(8,128)(2,1)S(1)}, u32[]{:S(2)}, u32[]{:S(2)}) collective-permute-start(bf16[130,16,128]{2,1,0:T(8,128)(2,1)S(1)} %get-tuple-element.16.refs_0_), channel_id=1, source_target_pairs={{0,64},{64,128},{128,192},{192,0},{1,65},{65,129},{129,193},{193,1... | collective-permute-start | bytes 1597448 | tf_op jit(solution)/shard_map/ppermute | solution.py:366
  10.8 20.7 %all-to-all-start = ((bf16[32,16,256]{2,1,0:T(8,128)(2,1)}), bf16[32,16,256]{2,1,0:T(8,128)(2,1)S(1)}, u32[]{:S(2)}, u32[]{:S(2)}) async-start(bf16[32,16,256]{2,1,0:T(8,128)(2,1)} %get-tuple-element.17), calls=%async_computation | async-start | bytes 524288 | tf_op jit(solution)/shard_map/all_to_all | solution.py:367
  21.8 15.7 %collective-permute-start = (bf16[130,16,128]{2,1,0:T(8,128)(2,1)S(1)}, bf16[130,16,128]{2,1,0:T(8,128)(2,1)}, u32[]{:S(2)}, u32[]{:S(2)}) collective-permute-start(bf16[130,16,128]{2,1,0:T(8,128)(2,1)S(1)} %get-tuple-element.16.refs_0_), channel_id=1, source_target_pairs={{0,32},{32,0},{1,33},{33,1},{2,34},{34,2},{3,35},{35,3},{4,36},{36... | collective-permute-start | bytes 1597448 | tf_op jit(solution)/shard_map/ppermute | solution.py:371
  33.3 5.5 %collective-permute-start.6 = (bf16[130,16,128]{2,1,0:T(8,128)(2,1)S(1)}, bf16[130,16,128]{2,1,0:T(8,128)(2,1)}, u32[]{:S(2)}, u32[]{:S(2)}) collective-permute-start(bf16[130,16,128]{2,1,0:T(8,128)(2,1)S(1)} %collective-permute-done.3.refs_6_.refs_0_), channel_id=1, source_target_pairs={{0,32},{32,0},{1,33},{33,1},{2,34},{34,2},{3,35},{35,3},{4,36},{36... | collective-permute-start | bytes 1597448 | tf_op jit(solution)/shard_map/ppermute | solution.py:371
  35.2 6.3 %collective-permute-start.4 = (bf16[130,16,128]{2,1,0:T(8,128)(2,1)S(1)}, bf16[130,16,128]{2,1,0:T(8,128)(2,1)S(1)}, u32[]{:S(2)}, u32[]{:S(2)}) collective-permute-start(bf16[130,16,128]{2,1,0:T(8,128)(2,1)S(1)} %collective-permute-done.1.refs_2_.refs_0_), channel_id=1, source_target_pairs={{0,32},{32,0},{1,33},{33,1},{2,34},{34,2},{3,35},{35,3},{4,36},{36... | collective-permute-start | bytes 1597448 | tf_op jit(solution)/shard_map/ppermute | solution.py:371
  35.3 6.2 %collective-permute-start.5 = (bf16[130,16,128]{2,1,0:T(8,128)(2,1)S(1)}, bf16[130,16,128]{2,1,0:T(8,128)(2,1)S(1)}, u32[]{:S(2)}, u32[]{:S(2)}) collective-permute-start(bf16[130,16,128]{2,1,0:T(8,128)(2,1)S(1)} %collective-permute-done.2.refs_4_.refs_2_), channel_id=1, source_target_pairs={{0,32},{32,0},{1,33},{33,1},{2,34},{34,2},{3,35},{35,3},{4,36},{36... | collective-permute-start | bytes 1597448 | tf_op jit(solution)/shard_map/ppermute | solution.py:371
  40.1 1.4 %copy-start = (bf16[2,2,128,16,128]{4,3,2,1,0:T(8,128)(2,1)}, bf16[2,2,128,16,128]{4,3,2,1,0:T(8,128)(2,1)S(1)}, u32[]{:S(2)}) copy-start(bf16[2,2,128,16,128]{4,3,2,1,0:T(8,128)(2,1)S(1)} %shift.5) | copy-start | bytes 6291460
where the time goes:
time: 103 us
  blocking collectives  45.2 us (44%)
  Pallas kernels  22.7 us (22%)
  starting transfers between devices  20.6 us (20%)
  waiting for transfers between devices  9.58 us (9%)
  local copies, waits for them, and re-layouts  3.49 us (3%)
    all_to_all x1, blocking collectives, body(): lax.all_to_all(parts.reshape(PLANE, ROWS, PIX), ('x', 'z'), 0, 0, tiled=T...  19 us
    all_to_all x1, blocking collectives, body(): images = lax.all_to_all(copies, ('x', 'z'), 0, 0, tiled=True)  14 us
    all_to_all x1, blocking collectives, body(): grads = lax.all_to_all(grads, ('y', 'core'), 0, 0, tiled=True)  12.2 us
    all_to_all x1, starting transfers between devices, body(): known = lax.all_to_all(known, ('x', 'z'), 0, 0, tiled=True)  11 us
    pallas_call x1, Pallas kernels, image_parts(): pl.pallas_call(image_kernel, out_shape=(jax.ShapeDtypeStruct((PLANE * ROW...  9.24 us
    all_to_all x1, waiting for transfers between devices, body(): known = lax.all_to_all(known, ('x', 'z'), 0, 0, tiled=True)  7.78 us
    ppermute x3, starting transfers between devices, body(): lax.ppermute(own, 'y', [(at, (at + back) % 4) for at in range(4)])  5.21 us
    pallas_call x3, Pallas kernels, shifted(): pl.pallas_call(functools.partial(shift_kernel, count), out_shape=jax.Shap...  5.05 us
  transfers between devices with their start and end apart: 8, of which 3 were waited for; matrix products, arithmetic and copies ran while one was open for 0% of the time, Pallas kernels for 4%

commit v1 on v0

v1 whole, which is shorter than its diff:
```python
import functools
import math

import jax
import jax.numpy as jnp
from jax import lax
from jax.experimental import pallas as pl
from jax.experimental.pallas import tpu as pltpu
from jax.sharding import Mesh, PartitionSpec as P

TAPS = 1024
RBINS = 16384
POLS = 4
SWATH = 512
PIX = 256
TILES = 256
GROUPS = 8
PLANE = 32
ROWS = 2 * POLS
BLOCK = 256
BLOCKS = RBINS // BLOCK
NOTE_ROWS = 16
EDGE = TAPS // BLOCK * ROWS
SPAN = TAPS + BLOCK
IMAGE_SCALE = 1.0 / math.sqrt(TILES * 2)
GRAD_SCALE = IMAGE_SCALE / math.sqrt(PIX * POLS)
VMEM_LIMIT = 14 * 1024 * 1024
BLOCK_ORDER = ((0, 0), (0, 1), (1, 0), (1, 1), (3, 0), (3, 1), (2, 0), (2, 1))
EARLY = 6
SMEM = pl.BlockSpec(memory_space=pltpu.SMEM)
VMEM = pl.BlockSpec(memory_space=pltpu.VMEM)
PARAMS = pltpu.CompilerParams(vmem_limit_bytes=VMEM_LIMIT)


def row_sign(shape, axis):
    return jnp.where(lax.broadcasted_iota(jnp.int32, shape, axis) < POLS, -1.0, 1.0)


def three_parts(x):
    first = x.astype(jnp.bfloat16).astype(jnp.float32)
    second = (x - first).astype(jnp.bfloat16).astype(jnp.float32)
    return [first, second, x - first - second]


def compress_kernel(
    raw_ref, taps_ref, error_ref, chosen_ref, start_ref, bins_ref, cross_ref, out_ref, known_ref, left_ref, odd_ref
):
    known = [bins_ref[...].astype(jnp.float32) - 256.0] + three_parts(cross_ref[...])
    known.append(jnp.zeros((5, PIX), jnp.float32))
    known = jnp.concatenate(known, axis=0).astype(jnp.bfloat16)
    for at in range(PLANE):
        known_ref[at] = known

    taps = taps_ref[...].astype(jnp.bfloat16).astype(jnp.float32)
    wide = []
    for part in range(2):
        rows = jnp.broadcast_to(taps[part : part + 1], (128, SPAN))
        rows = pltpu.roll(rows, 0, 1, stride=1, stride_axis=0).astype(jnp.bfloat16)
        later = jnp.concatenate([jnp.zeros((128, 128), jnp.bfloat16), rows[:, : SPAN - 128]], axis=1)
        wide.append(jnp.concatenate([rows, later], axis=0))

    total = BLOCKS * ROWS
    stride = total + EDGE
    for pulse in range(2):
        own = raw_ref[pulse * total : (pulse + 1) * total]
        edge = jnp.zeros((EDGE + ROWS, BLOCK), jnp.float32)
        at = pulse * stride
        left_ref[at : at + total] = own
        left_ref[at + total : at + stride] = edge[ROWS:].astype(jnp.bfloat16)
        odd_ref[at : at + stride] = jnp.concatenate([own.astype(jnp.float32)[ROWS:], edge], axis=0).astype(jnp.bfloat16)
    shifted = []
    for j in range(SPAN // BLOCK):
        source = odd_ref if j % 2 else left_ref
        at = j // 2 * 2 * ROWS
        shifted.append(source[at : at + stride + total])
    sums = lax.dot_general(
        jnp.concatenate(shifted, axis=1),
        jnp.concatenate(wide, axis=0),
        (((1,), (1,)), ((), ())),
        preferred_element_type=jnp.float32,
    )
    for pulse in range(2):
        done = sums[pulse * stride : pulse * stride + total].reshape(BLOCKS, ROWS, 2 * BLOCK)
        crossed = pltpu.roll(done[:, :, BLOCK:], POLS, 1) * -row_sign((BLOCKS, ROWS, BLOCK), 1)
        done = done[:, :, :BLOCK] + crossed
        out_ref[pulse * BLOCKS : (pulse + 1) * BLOCKS] = jnp.concatenate(
            [done[:, :, :128], done[:, :, 128:]], axis=1
        ).astype(jnp.bfloat16)

    rows = [chosen_ref[...].astype(jnp.float32), start_ref[...].astype(jnp.float32)]
    for pulse in range(2):
        rows += three_parts(jnp.full((1, PIX), error_ref[pulse], jnp.float32))
    rows.append(jnp.zeros((NOTE_ROWS - 10, PIX), jnp.float32))
    rows = jnp.concatenate(rows, axis=0).astype(jnp.bfloat16)
    out_ref[2 * BLOCKS] = rows[:, :128]
    out_ref[2 * BLOCKS + 1] = rows[:, 128:]


def compress(raw, taps, phase_error, chosen, start, bins, cross):
    return pl.pallas_call(
        compress_kernel,
        out_shape=(
            jax.ShapeDtypeStruct((2 * BLOCKS + 2, 2 * ROWS, 128), jnp.bfloat16),
            jax.ShapeDtypeStruct((PLANE, 16, PIX), jnp.bfloat16),
        ),
        in_specs=[VMEM, VMEM, SMEM, VMEM, VMEM, VMEM, VMEM],
        out_specs=(VMEM, VMEM),
        scratch_shapes=[
            pltpu.VMEM((2 * (BLOCKS * ROWS + EDGE), BLOCK), jnp.bfloat16),
            pltpu.VMEM((2 * (BLOCKS * ROWS + EDGE), BLOCK), jnp.bfloat16),
        ],
        compiler_params=PARAMS,
        name="compress",
    )(raw, taps, phase_error, chosen, start, bins, cross)


def halves_kernel(near_ref, far_ref, first_ref, second_ref):
    first_ref[...] = near_ref[:BLOCKS]
    second_ref[...] = far_ref[BLOCKS:]


def halves(near, far):
    return pl.pallas_call(
        halves_kernel,
        out_shape=(
            jax.ShapeDtypeStruct((BLOCKS, 2 * ROWS, 128), jnp.bfloat16),
            jax.ShapeDtypeStruct((BLOCKS + 2, 2 * ROWS, 128), jnp.bfloat16),
        ),
        in_specs=[VMEM, VMEM],
        out_specs=(VMEM, VMEM),
        compiler_params=PARAMS,
        name="halves",
    )(near, far)


def pieces(refs):
    if len(refs) == 1:
        return [(refs[0], 0), (refs[0], BLOCKS), (refs[0], 2 * BLOCKS)]
    return [(refs[0], 0), (refs[1], 0), (refs[1], BLOCKS)]


def write_pairs(blocks, comp_ref):
    size = 2 * BLOCKS
    for dev, block in enumerate(blocks):
        for pulse in range(2):
            ref, place = block[pulse]
            at = dev * 2 * size + pulse * BLOCKS
            comp_ref[at : at + BLOCKS] = ref[place : place + BLOCKS]
            rows = ref[place : place + BLOCKS].astype(jnp.float32)
            later = jnp.concatenate([rows[1:, :ROWS], rows[:1, :ROWS]], axis=0)
            at = at + size
            comp_ref[at : at + BLOCKS] = jnp.concatenate([rows[:, ROWS:], later], axis=1).astype(jnp.bfloat16)


def kappa_turns(bins):
    turned = 31.0 * bins
    left = turned - 97.0 * jnp.floor((turned + 0.5) * (1.0 / 97.0))
    return left * (1.0 / 97.0)


def cos_sin(turns):
    quarter = jnp.floor(4.0 * turns + 0.5)
    angle = (turns - 0.25 * quarter) * (2.0 * math.pi)
    square = angle * angle
    cosine = 1.0 + square * (-1 / 2 + square * (1 / 24 + square * (-1 / 720 + square * (1 / 40320))))
    sine = 1.0 + square * (-1 / 6 + square * (1 / 120 + square * (-1 / 5040 + square * (1 / 362880))))
    sine = angle * sine
    quarter = quarter.astype(jnp.int32)
    crossed = (quarter & 1) != 0
    first = jnp.where(crossed, sine, cosine)
    second = jnp.where(crossed, cosine, sine)
    first = jnp.where(((quarter + 1) & 2) != 0, -first, first)
    second = jnp.where((quarter & 2) != 0, -second, second)
    return first, second


def write_lists(group, blocks, whole_ref, turn_ref):
    count = len(blocks)
    notes = [
        jnp.concatenate([ref[place], ref[place + 1]], axis=1).astype(jnp.float32) for _, _, (ref, place) in blocks
    ]
    homes = jnp.concatenate([jnp.full((1, PIX), at * 4.0 * BLOCKS, jnp.float32) for at in range(count)], axis=0)
    rows, chosen, cosines, sines = [], [], [], []
    for slot in range(2):
        pulse = jnp.concatenate([note[slot : slot + 1] for note in notes], axis=0)
        start = jnp.concatenate([note[2 + slot : 3 + slot] for note in notes], axis=0)
        errors = [
            jnp.concatenate([note[at : at + 1] + note[at + 1 : at + 2] + note[at + 2 : at + 3] for note in notes], axis=0)
            for at in (4, 7)
        ]
        errors = jnp.where(pulse < 0.5, errors[0], errors[1]) * (0.5 / math.pi)
        cosine, sine = cos_sin(kappa_turns(128.0 * start) - errors)
        filled = pulse < 1.5
        pair = jnp.floor(0.5 * start)
        rows.append((2.0 * (start - 2.0 * pair) + jnp.minimum(pulse, 1.0)) * BLOCKS + pair + homes)
        chosen.append(pulse)
        cosines.append(jnp.where(filled, cosine, 0.0))
        sines.append(jnp.where(filled, sine, 0.0))
    shift = (TILES - group * PLANE) % TILES
    for parts, ref in ((rows + chosen, whole_ref), (cosines + sines, turn_ref)):
        parts = jnp.concatenate(parts + [jnp.zeros((128 - 4 * count, TILES), jnp.float32)], axis=0)
        parts = pltpu.roll(parts, shift, 1)[:, :128]
        ref[...] = parts.T[:PLANE].astype(ref.dtype)


def phase_kernel(group_ref, rate_ref, known_ref, bins_ref, phase_ref, facts_ref):
    facts_ref[...] = jnp.swapaxes(known_ref[...].astype(jnp.float32), 0, 1)
    cross = facts_ref[8] + facts_ref[9] + facts_ref[10]
    for dev in range(GROUPS):
        bins = facts_ref[group_ref[dev]] + 256.0
        phase_ref[dev, 0], phase_ref[dev, 1] = cos_sin(kappa_turns(bins) + rate_ref[dev] * cross)
        bins_ref[dev] = bins.astype(jnp.int32)


def phases(groups, rates, known):
    return pl.pallas_call(
        phase_kernel,
        out_shape=(
            jax.ShapeDtypeStruct((GROUPS, PLANE, PIX), jnp.int32),
            jax.ShapeDtypeStruct((GROUPS, 2, PLANE, PIX), jnp.float32),
        ),
        in_specs=[SMEM, SMEM, VMEM],
        out_specs=(VMEM, VMEM),
        scratch_shapes=[pltpu.VMEM((16, PLANE, PIX), jnp.float32)],
        compiler_params=PARAMS,
        cost_estimate=pl.CostEstimate(flops=1_200_000_000, bytes_accessed=1_000_000, transcendentals=0),
        name="phases",
    )(groups, rates, known)


def pick_lanes(rows, lanes):
    dims = lax.GatherDimensionNumbers(
        offset_dims=(),
        collapsed_slice_dims=(1,),
        start_index_map=(1,),
        operand_batching_dims=(0,),
        start_indices_batching_dims=(0,),
    )
    return lax.gather(rows, lanes[..., None], dims, slice_sizes=(1, 1), mode="promise_in_bounds")


def image_kernel(first, count, parts, last, group_ref, bins_ref, phase_ref, *refs):
    blocks = [pieces(refs[at * parts : (at + 1) * parts]) for at in range(count)]
    refs = refs[count * parts :]
    if first:
        before_ref, refs = refs[0], refs[1:]
    part_ref, kept_ref, lists_ref, comp_ref, turns_ref, whole_ref, turn_ref, sems, *rest = refs
    sum_ref = rest[0] if last else part_ref
    write_lists(group_ref[0], blocks, lists_ref, turns_ref)
    copies = [
        pltpu.make_async_copy(lists_ref, whole_ref, sems.at[0]),
        pltpu.make_async_copy(turns_ref, turn_ref, sems.at[1]),
    ]
    for copy in copies:
        copy.start()
    write_pairs(blocks, comp_ref)
    for copy in copies:
        copy.wait()
    sign = row_sign((ROWS, 128), 0)

    def step(tile, carry):
        total = [before_ref[tile, :, :128], before_ref[tile, :, 128:]] if first else [None, None]
        for at in range(count):
            dev = first + at
            bins = bins_ref[dev, pl.ds(tile, 1), :]
            cos_row = phase_ref[dev, 0, pl.ds(tile, 1), :]
            sin_row = phase_ref[dev, 1, pl.ds(tile, 1), :]
            sources = []
            for slot in range(2):
                base = whole_ref[tile, slot * count + at]
                sources.append((comp_ref[base], comp_ref[base + 1]))
            cos_rot = [turn_ref[tile, slot * count + at] for slot in range(2)]
            sin_rot = [turn_ref[tile, (2 + slot) * count + at] * sign for slot in range(2)]
            for half in range(2):
                lanes = slice(half * 128, (half + 1) * 128)
                where = jnp.broadcast_to(bins[:, lanes], (ROWS, 128))
                lane = where & 127
                odd = (where & 128) != 0
                high = (where & 256) != 0
                lane = jnp.concatenate([lane, lane], axis=0).astype(jnp.int16)
                turned = []
                for slot in range(2):
                    low, top = [pick_lanes(source, lane).astype(jnp.float32) for source in sources[slot]]
                    value = jnp.where(
                        high, jnp.where(odd, top[ROWS:], top[:ROWS]), jnp.where(odd, low[ROWS:], low[:ROWS])
                    )
                    turned.append(cos_rot[slot] * value + sin_rot[slot] * pltpu.roll(value, POLS, 0))
                turned = jnp.concatenate(turned, axis=0).astype(jnp.bfloat16)
                kept_ref[tile, at, :, lanes] = turned
                turned = turned.astype(jnp.float32)
                summed = turned[:ROWS] + turned[ROWS:]
                term = jnp.broadcast_to(cos_row[:, lanes], (ROWS, 128)) * summed + jnp.broadcast_to(
                    sin_row[:, lanes], (ROWS, 128)
                ) * (sign * pltpu.roll(summed, POLS, 0))
                total[half] = term if total[half] is None else total[half] + term
        sum_ref[tile] = jnp.concatenate(total, axis=1)
        return carry

    lax.fori_loop(0, PLANE, step, 0, unroll=8 if last else 4)
    if last:
        part_ref[...] = sum_ref[...].reshape(PLANE * ROWS, PIX).astype(jnp.bfloat16)


def image_parts(first, group, bins, phase, pulses, before=()):
    count, parts = len(pulses), len(pulses[0])
    pulses = [piece for block in pulses for piece in block]
    last = first + count == GROUPS
    part = ((PLANE * ROWS, PIX), jnp.bfloat16) if last else ((PLANE, ROWS, PIX), jnp.float32)
    return pl.pallas_call(
        functools.partial(image_kernel, first, count, parts, last),
        out_shape=(
            jax.ShapeDtypeStruct(*part),
            jax.ShapeDtypeStruct((PLANE, count, 2 * ROWS, PIX), jnp.bfloat16),
            jax.ShapeDtypeStruct((PLANE, 128), jnp.int32),
        ),
        in_specs=[SMEM] + [VMEM] * (2 + len(pulses) + len(before)),
        out_specs=(VMEM, VMEM, VMEM),
        scratch_shapes=[
            pltpu.VMEM((count * 4 * BLOCKS, 2 * ROWS, 128), jnp.bfloat16),
            pltpu.VMEM((PLANE, 128), jnp.float32),
            pltpu.SMEM((PLANE, 128), jnp.int32),
            pltpu.SMEM((PLANE, 128), jnp.float32),
            pltpu.SemaphoreType.DMA((2,)),
        ]
        + ([pltpu.VMEM((PLANE, ROWS, PIX), jnp.float32)] if last else []),
        compiler_params=PARAMS,
        cost_estimate=pl.CostEstimate(flops=100_000_000 * count, bytes_accessed=1_000_000, transcendentals=0),
        name="image",
    )(group, bins, phase, *pulses, *before)


def total_kernel(parts_ref, tile_ref, copies_ref):
    image = IMAGE_SCALE * jnp.sum(parts_ref[...].astype(jnp.float32), axis=0)
    for row in range(ROWS):
        tile_ref[row % POLS, row // POLS, :] = image[row]
    for at in range(PLANE):
        copies_ref[at] = image


def total_image(parts):
    return pl.pallas_call(
        total_kernel,
        out_shape=(
            jax.ShapeDtypeStruct((POLS, 2, PIX), jnp.float32),
            jax.ShapeDtypeStruct((PLANE, ROWS, PIX), jnp.float32),
        ),
        in_specs=[VMEM],
        out_specs=(VMEM, VMEM),
        compiler_params=PARAMS,
        name="total",
    )(parts)


def grad_kernel(group_ref, whole_a, whole_b, image_ref, kept_a, kept_b, phase_ref, out_ref):
    sign = row_sign((ROWS, 128), 0)

    def step(tile, sums):
        sums = list(sums)
        firsts, seconds = [], []
        for half in range(2):
            image = image_ref[tile, :, half * 128 : (half + 1) * 128]
            other = pltpu.roll(image, POLS, 0)
            size = 4.0 * (image * image + other * other)
            firsts.append(size * image)
            seconds.append((size * other) * sign)
        for dev in range(GROUPS):
            cos_row = phase_ref[dev, 0, pl.ds(tile, 1), :]
            sin_row = phase_ref[dev, 1, pl.ds(tile, 1), :]
            weights = []
            for half in range(2):
                lanes = slice(half * 128, (half + 1) * 128)
                weights.append(
                    firsts[half] * jnp.broadcast_to(sin_row[:, lanes], (ROWS, 128))
                    + seconds[half] * jnp.broadcast_to(cos_row[:, lanes], (ROWS, 128))
                )
            whole_ref, kept_ref, at = (whole_a, kept_a, dev) if dev < EARLY else (whole_b, kept_b, dev - EARLY)
            count = EARLY if dev < EARLY else GROUPS - EARLY
            kept = kept_ref[tile, at].astype(jnp.float32)
            for slot in range(2):
                value = kept[slot * ROWS : (slot + 1) * ROWS]
                term = weights[0] * value[:, :128] + weights[1] * value[:, 128:]
                pulse = whole_ref[tile, (2 + slot) * count + at]
                for which in range(2):
                    home = dev * 2 + which
                    sums[home] = sums[home] + jnp.where(pulse == which, 1.0, 0.0) * term
        return tuple(sums)

    zero = jnp.zeros((ROWS, 128), jnp.float32)
    sums = lax.fori_loop(0, PLANE, step, (zero,) * (2 * GROUPS), unroll=4)
    rows = jnp.concatenate([jnp.sum(part, axis=0, keepdims=True) for part in sums], axis=0)
    totals = jnp.sum(rows, axis=1, keepdims=True) * GRAD_SCALE
    lane = lax.broadcasted_iota(jnp.int32, (1, 128), 1)
    for dev in range(GROUPS):
        out_ref[group_ref[dev]] = jnp.where(lane == 0, totals[2 * dev : 2 * dev + 1], totals[2 * dev + 1 : 2 * dev + 2])


def grad_parts(groups, wholes, image, kepts, phase):
    return pl.pallas_call(
        grad_kernel,
        out_shape=jax.ShapeDtypeStruct((GROUPS, 1, 128), jnp.float32),
        in_specs=[SMEM, SMEM, SMEM] + [VMEM] * 4,
        out_specs=VMEM,
        compiler_params=PARAMS,
        name="grad",
    )(groups, *wholes, image, *kepts, phase)


def body(raw_pulses, chirp_taps, phase_error, illumination, swath_start, range_bins, cross_range):
    core = lax.axis_index("core")
    at_y = lax.axis_index("y")
    at_plane = lax.axis_index(("x", "z"))
    groups = jnp.stack([2 * ((at_y + 4 - back) % 4) + (core + other) % 2 for back, other in BLOCK_ORDER])
    rates = (2 * (groups * PLANE + at_plane) + 1 - TILES).astype(jnp.float32) / (2 * TILES)

    raw = raw_pulses.reshape(2, POLS, 2, BLOCKS, BLOCK).transpose(0, 3, 2, 1, 4)
    own, known = compress(
        raw.reshape(2 * BLOCKS * ROWS, BLOCK),
        jnp.pad(chirp_taps, ((0, 0), (0, SPAN - TAPS))),
        phase_error,
        illumination[0].T,
        swath_start[0].T,
        range_bins[0],
        cross_range,
    )
    def back_by(x, steps):
        return lax.ppermute(x, "y", [(at, (at + steps) % 4) for at in range(4)])

    def pair(*block):
        return [block, tuple(lax.ppermute(x, "core", [(0, 1), (1, 0)]) for x in block)]

    near, far = back_by(own, 1), back_by(own, 3)
    first, second = halves(near, far)
    across = (back_by(first, 1), back_by(second, 3))
    known = lax.all_to_all(known, ("x", "z"), 0, 0, tiled=True)
    bins, phase = phases(groups, rates, known)
    before, kept_a, whole_a = image_parts(0, groups[:1], bins, phase, pair(own) + pair(near) + pair(far))
    across = lax.optimization_barrier((*across, before))[:2]
    parts, kept_b, whole_b = image_parts(EARLY, groups[:1], bins, phase, pair(*across), (before,))
    parts = lax.all_to_all(parts.reshape(PLANE, ROWS, PIX), ("x", "z"), 0, 0, tiled=True)
    image_tile, copies = total_image(parts)
    images = lax.all_to_all(copies, ("x", "z"), 0, 0, tiled=True)
    grads = grad_parts(groups, (whole_a, whole_b), images, (kept_a, kept_b), phase)
    grads = lax.all_to_all(grads, ("y", "core"), 0, 0, tiled=True)
    return (image_tile[None], jnp.sum(grads[:, 0, :2], axis=0))


def solution(mesh):
    fine = Mesh(mesh.devices.reshape(4, 2, 4, 8), ("y", "core", "x", "z"))
    every = ("y", "core", "x", "z")
    return jax.shard_map(
        body,
        mesh=fine,
        in_specs=(
            P(every, None, None, None),
            P(),
            P(every),
            P(every, None, None),
            P(every, None, None),
            P(every, None, None),
            P(every, None),
        ),
        out_specs=(P(every, None, None, None), P(every)),
        check_vma=False,
    )
```

time: 103 us -> 89.9 us (0.87)
  Pallas kernels: 22.7 us -> 16.9 us
  blocking collectives: 45.2 us -> 40.4 us
  waiting for transfers between devices: 9.58 us -> 5.83 us
  starting transfers between devices: 20.6 us -> 23.1 us
  local copies, waits for them, and re-layouts: 3.49 us -> 2.06 us
    pallas_call x6 -> x4, Pallas kernels: 17.5 us -> 11.8 us  [the longest x2 8.55 us: image_parts(): pl.pallas_call(functools.partial(image_kernel, first, count, parts, last)...]
    all_to_all x1, waiting for transfers between devices: 7.78 us -> 4.15 us  [body(): known = lax.all_to_all(known, ('x', 'z'), 0, 0, tiled=True)]
    all_to_all x1, blocking collectives: 19 us -> 16 us  [body(): lax.all_to_all(parts.reshape(PLANE, ROWS, PIX), ('x', 'z'), 0, 0, tiled=T...]
    ppermute x7 -> x9, starting transfers between devices: 9.52 us -> 11.9 us  [the longest x4 6.06 us: back_by(): return lax.ppermute(x, 'y', [(at, (at + steps) % 4) for at in range(4)])]
    all_to_all x1, blocking collectives: 12.2 us -> 10.5 us  [body(): grads = lax.all_to_all(grads, ('y', 'core'), 0, 0, tiled=True)]
    unnamed x14 -> x12, local copies, waits for them, and re-layouts: 1.38 us -> 0.03 us
  transfers between devices with their start and end apart: 8 -> 10, of which waited for: 3 -> 2; matrix products, arithmetic and copies ran while one was open for 0% -> 0% of each run, Pallas kernels for 4% -> 8%
where the time goes in v1:
time: 89.9 us; the launch traced here: 89.5 us
  blocking collectives  40.4 us (45%)
  starting transfers between devices  23.1 us (26%)
  Pallas kernels  16.9 us (19%)
  waiting for transfers between devices  5.83 us (6%)
  local copies, waits for them, and re-layouts  2.06 us (2%)
    all_to_all x1, blocking collectives, body(): lax.all_to_all(parts.reshape(PLANE, ROWS, PIX), ('x', 'z'), 0, 0, tiled=T...  16 us
    all_to_all x1, blocking collectives, body(): images = lax.all_to_all(copies, ('x', 'z'), 0, 0, tiled=True)  13.8 us
    all_to_all x1, starting transfers between devices, body(): known = lax.all_to_all(known, ('x', 'z'), 0, 0, tiled=True)  11.2 us
    all_to_all x1, blocking collectives, body(): grads = lax.all_to_all(grads, ('y', 'core'), 0, 0, tiled=True)  10.5 us
    pallas_call x2, Pallas kernels, image_parts(): pl.pallas_call(functools.partial(image_kernel, first, count, parts, last)...  8.55 us
    ppermute x4, starting transfers between devices, back_by(): return lax.ppermute(x, 'y', [(at, (at + steps) % 4) for at in range(4)])  6.06 us
    ppermute x5, starting transfers between devices, pair(): lax.ppermute(x, 'core', [(0, 1), (1, 0)])  5.83 us
    all_to_all x1, waiting for transfers between devices, body(): known = lax.all_to_all(known, ('x', 'z'), 0, 0, tiled=True)  4.15 us
  transfers between devices with their start and end apart: 10, of which 2 were waited for; matrix products, arithmetic and copies ran while one was open for 0% of the time, Pallas kernels for 8%

profile of v1, /device:TPU:1, one launch (start us, length us, event | category | flops | bytes accessed | tf_op | source)
XLA Modules:
  0.0 89.5 jit_solution(4850403189686236190)
XLA Ops:
  0.6 0.0 copy-start.5
  0.6 0.0 copy-start.1
  0.7 0.0 copy-start.2
  0.7 0.0 copy-start
  0.7 0.0 copy-start.3
  0.7 0.0 copy-start.4
  0.7 1.4 %reshape.13 = bf16[2,4,2,64,256]{4,3,2,1,0:T(8,128)(2,1)S(1)} reshape(bf16[2,4,2,16384]{3,2,1,0:T(2,128)(2,1)} %param.7) | data formatting | bytes 1048576 | tf_op jit(solution)/shard_map/reshape | solution.py:415
  2.1 0.4 copy.11
  2.5 0.1 reshape.14.raw_ref
  2.6 0.0 copy-done.5
  2.7 0.0 copy-done.1
  2.7 0.0 copy-done.2
  2.7 0.0 copy-done
  2.7 0.0 copy-done.3
  2.7 0.0 copy-done.4
  2.7 2.9 %compress.1 = (bf16[130,16,128]{2,1,0:T(8,128)(2,1)S(1)}, bf16[32,16,256]{2,1,0:T(8,128)(2,1)}) custom-call(bf16[1024,256]{1,0:T(8,128)(2,1)S(1)} %reshape.14.raw_ref, f32[2,1280]{1,0:T(2,128)S(1)} %pad.4.taps_ref, f32[2]{0:T(128)S(1)} %copy-done.4, s32[2,256]{1,0:T(2,128)S(1)} %bitcast.22, s32[2,256]{1,0:T(2,128)S(1)} %bitcast.23, s32[8,256]{1,0:T(8,128)S(1)} %bitcast.21, ...), custom_call_target="tpu_custom_call" | custom-call | tf_op jit(solution)/shard_map/compress/pallas_call | solution.py:100
  5.6 2.1 %collective-permute-start = (bf16[130,16,128]{2,1,0:T(8,128)(2,1)S(1)}, bf16[130,16,128]{2,1,0:T(8,128)(2,1)S(1)}, u32[]{:S(2)}, u32[]{:S(2)}) collective-permute-start(bf16[130,16,128]{2,1,0:T(8,128)(2,1)S(1)} %get-tuple-element.21.refs_0_), channel_id=1, source_target_pairs={{0,64},{64,128},{128,192},{192,0},{1,65},{65,129},{129,193},{193,1... | collective-permute-start | bytes 1597448 | tf_op jit(solution)/shard_map/ppermute | solution.py:426
  7.7 1.4 %collective-permute-start.1 = (bf16[130,16,128]{2,1,0:T(8,128)(2,1)S(1)}, bf16[130,16,128]{2,1,0:T(8,128)(2,1)S(1)}, u32[]{:S(2)}, u32[]{:S(2)}) collective-permute-start(bf16[130,16,128]{2,1,0:T(8,128)(2,1)S(1)} %get-tuple-element.21.refs_0_), channel_id=1, source_target_pairs={{0,192},{64,0},{128,64},{192,128},{1,193},{65,1},{129,65},{193,129... | collective-permute-start | bytes 1597448 | tf_op jit(solution)/shard_map/ppermute | solution.py:426
  9.2 11.2 %all-to-all-start = ((bf16[32,16,256]{2,1,0:T(8,128)(2,1)}), bf16[32,16,256]{2,1,0:T(8,128)(2,1)}, u32[]{:S(2)}, u32[]{:S(2)}) async-start(bf16[32,16,256]{2,1,0:T(8,128)(2,1)} %get-tuple-element.18), calls=%async_computation | async-start | bytes 524288 | tf_op jit(solution)/shard_map/all_to_all | solution.py:434
  20.4 1.5 %collective-permute-start.4 = (bf16[130,16,128]{2,1,0:T(8,128)(2,1)S(1)}, bf16[130,16,128]{2,1,0:T(8,128)(2,1)S(1)}, u32[]{:S(2)}, u32[]{:S(2)}) collective-permute-start(bf16[130,16,128]{2,1,0:T(8,128)(2,1)S(1)} %get-tuple-element.21.refs_0_), channel_id=1, source_target_pairs={{0,32},{32,0},{1,33},{33,1},{2,34},{34,2},{3,35},{35,3},{4,36},{36... | collective-permute-start | bytes 1597448 | tf_op jit(solution)/shard_map/ppermute | solution.py:429
  21.9 0.0 collective-permute-done.near_ref.refs_2_
  21.9 0.3 collective-permute-start.5
  22.2 0.0 collective-permute-done.1.far_ref.refs_4_
  22.2 0.2 collective-permute-start.6
  22.4 0.1 stack.35.group_ref
  22.5 0.8 halves.1
  23.3 2.5 %collective-permute-start.3 = (bf16[66,16,128]{2,1,0:T(8,128)(2,1)}, bf16[66,16,128]{2,1,0:T(8,128)(2,1)S(1)}, u32[]{:S(2)}, u32[]{:S(2)}) collective-permute-start(bf16[66,16,128]{2,1,0:T(8,128)(2,1)} %get-tuple-element.23), channel_id=1, source_target_pairs={{0,192},{64,0},{128,64},{192,128},{1,193},{65,1},{129,65},{193,129... | collective-permute-start | bytes 811016 | tf_op jit(solution)/shard_map/ppermute | solution.py:426
  25.8 0.0 collective-permute-start.2
  25.8 4.1 %all-to-all-done.known_ref = bf16[32,16,256]{2,1,0:T(8,128)(2,1)} async-done(((bf16[32,16,256]{2,1,0:T(8,128)(2,1)}), bf16[32,16,256]{2,1,0:T(8,128)(2,1)}, u32[]{:S(2)}, u32[]{:S(2)}) %all-to-all-start) | async-done | bytes 262176 | tf_op jit(solution)/shard_map/all_to_all | solution.py:434
  30.0 1.5 %phases.1 = (s32[8,32,256]{2,1,0:T(8,128)S(1)}, f32[8,2,32,256]{3,2,1,0:T(8,128)S(1)}) custom-call(s32[8]{0:T(128)S(1)} %stack.35.group_ref, f32[8]{0:T(128)S(1)} %convert_multiply_fusion.rate_ref, bf16[32,16,256]{2,1,0:T(8,128)(2,1)} %all-to-all-done.known_ref), custom_call_target="tpu_custom_call" | custom-call | flops 1200000000 | bytes 1000000 | tf_op jit(solution)/shard_map/phases/pallas_call | solution.py:216
  31.5 0.0 collective-permute-done.4.refs_1_
  31.6 0.0 collective-permute-done.5.refs_3_
  31.6 0.0 collective-permute-done.6.refs_5_
  31.6 4.8 %image.2 = (f32[32,8,256]{2,1,0:T(8,128)S(1)}, bf16[32,6,16,256]{3,2,1,0:T(8,128)(2,1)S(1)}, s32[32,128]{1,0:T(8,128)S(1)}) custom-call(s32[1]{0:T(128)} %bitcast.group_ref, s32[8,32,256]{2,1,0:T(8,128)S(1)} %get-tuple-element.19.bins_ref, f32[8,2,32,256]{3,2,1,0:T(8,128)S(1)} %get-tuple-element.20.phase_ref, ...), custom_call_target="tpu_custom_call" | custom-call | flops 600000000 | bytes 1000000 | tf_op jit(solution)/shard_map/image/pallas_call | solution.py:309
  36.4 0.0 collective-permute-done.2.refs_0_
  36.4 0.0 collective-permute-done.3.refs_1_
  36.4 3.7 %collective-permute-start.8 = (bf16[66,16,128]{2,1,0:T(8,128)(2,1)S(1)}, bf16[66,16,128]{2,1,0:T(8,128)(2,1)S(1)}, u32[]{:S(2)}, u32[]{:S(2)}) collective-permute-start(bf16[66,16,128]{2,1,0:T(8,128)(2,1)S(1)} %collective-permute-done.3.refs_1_), channel_id=1, source_target_pairs={{0,32},{32,0},{1,33},{33,1},{2,34},{34,2},{3,35},{35,3},{4,36},{36... | collective-permute-start | bytes 811016 | tf_op jit(solution)/shard_map/ppermute | solution.py:429
  40.1 0.1 collective-permute-start.7
  40.2 1.7 %collective-permute-done.7.refs_2_ = bf16[64,16,128]{2,1,0:T(8,128)(2,1)S(1)} collective-permute-done((bf16[64,16,128]{2,1,0:T(8,128)(2,1)}, bf16[64,16,128]{2,1,0:T(8,128)(2,1)S(1)}, u32[]{:S(2)}, u32[]{:S(2)}) %collective-permute-start.7) | collective-permute-done | bytes 262176 | tf_op jit(solution)/shard_map/ppermute | solution.py:429
  41.8 0.0 collective-permute-done.8.refs_3_
  41.8 3.8 %image.3 = (bf16[256,256]{1,0:T(8,128)(2,1)S(1)}, bf16[32,2,16,256]{3,2,1,0:T(8,128)(2,1)S(1)}, s32[32,128]{1,0:T(8,128)S(1)}) custom-call(s32[1]{0:T(128)} %bitcast.group_ref, s32[8,32,256]{2,1,0:T(8,128)S(1)} %get-tuple-element.19.bins_ref, f32[8,2,32,256]{3,2,1,0:T(8,128)S(1)} %get-tuple-element.20.phase_ref, ...), custom_call_target="tpu_custom_call" | custom-call | flops 200000000 | bytes 1000000 | tf_op jit(solution)/shard_map/image/pallas_call | solution.py:309
  45.6 16.0 %all_to_all.20.parts_ref = bf16[32,8,256]{2,1,0:T(8,128)(2,1)S(1)} all-to-all(bf16[32,8,256]{2,1,0:T(8,128)(2,1)S(1)} %bitcast.20), channel_id=1, replica_groups=mesh['y'=4,'core'=2,'x'=4,'z'=8] {'x','z'}, dimensions={0} | all-to-all | bytes 262144 | tf_op jit(solution)/shard_map/all_to_all | solution.py:439
  61.6 0.7 total.1
  62.3 13.8 %all_to_all.21.image_ref = f32[32,8,256]{2,1,0:T(8,128)S(1)} all-to-all(f32[32,8,256]{2,1,0:T(8,128)S(1)} %get-tuple-element.31), channel_id=1, replica_groups=mesh['y'=4,'core'=2,'x'=4,'z'=8] {'x','z'}, dimensions={0} | all-to-all | bytes 524288 | tf_op jit(solution)/shard_map/all_to_all | solution.py:441
  76.1 2.4 %grad.1 = f32[8,1,128]{2,1,0:T(1,128)S(1)} custom-call(s32[8]{0:T(128)S(1)} %stack.35.group_ref, s32[32,128]{1,0:T(8,128)S(1)} %get-tuple-element.29.whole_a, s32[32,128]{1,0:T(8,128)S(1)} %get-tuple-element.30.whole_b, f32[32,8,256]{2,1,0:T(8,128)S(1)} %all_to_all.21.image_ref, bf16[32,6,16,256]{3,2,1,0:T(8,128)(2,1)S(1)} %get-tuple-element.32.kept_a, ...), custom_call_target="tpu_custom_call" | custom-call | tf_op jit(solution)/shard_map/grad/pallas_call | solution.py:398
  78.4 10.5 %all_to_all.22 = f32[8,1,128]{2,1,0:T(1,128)S(1)} all-to-all(f32[8,1,128]{2,1,0:T(1,128)S(1)} %grad.1), channel_id=1, replica_groups=mesh['y'=4,'core'=2,'x'=4,'z'=8] {'y','core'}, dimensions={0} | all-to-all | bytes 8192 | tf_op jit(solution)/shard_map/all_to_all | solution.py:443
  89.0 0.5 slice_reduce_fusion
  (2 shorter events, 0.0 us)
Async XLA Ops:
  0.6 2.0 %copy-start.5 = (f32[2,1024]{1,0:T(2,128)S(1)}, f32[2,1024]{1,0:T(2,128)}, u32[]{:S(2)}) copy-start(f32[2,1024]{1,0:T(2,128)} %param.8) | copy-start | bytes 24580
  0.6 2.0 %copy-start.1 = (s32[1,256,2]{1,2,0:T(2,128)S(1)}, s32[1,256,2]{1,2,0:T(2,128)}, u32[]{:S(2)}) copy-start(s32[1,256,2]{1,2,0:T(2,128)} %param.10) | copy-start | bytes 6148
  0.7 2.0 %copy-start.2 = (s32[1,256,2]{1,2,0:T(2,128)S(1)}, s32[1,256,2]{1,2,0:T(2,128)}, u32[]{:S(2)}) copy-start(s32[1,256,2]{1,2,0:T(2,128)} %param.11) | copy-start | bytes 6148
  0.7 2.0 %copy-start = (s32[1,8,256]{2,1,0:T(8,128)S(1)}, s32[1,8,256]{2,1,0:T(8,128)}, u32[]{:S(2)}) copy-start(s32[1,8,256]{2,1,0:T(8,128)} %param.12) | copy-start | bytes 24580
  0.7 2.0 %copy-start.3 = (f32[1,256]{1,0:T(1,128)S(1)}, f32[1,256]{1,0:T(1,128)}, u32[]{:S(2)}) copy-start(f32[1,256]{1,0:T(1,128)} %cross_ref.1) | copy-start | bytes 3076
  0.7 2.0 %copy-start.4 = (f32[2]{0:T(128)S(1)}, f32[2]{0:T(128)}, u32[]{:S(2)}) copy-start(f32[2]{0:T(128)} %error_ref.1) | copy-start | bytes 28
  5.6 16.3 %collective-permute-start = (bf16[130,16,128]{2,1,0:T(8,128)(2,1)S(1)}, bf16[130,16,128]{2,1,0:T(8,128)(2,1)S(1)}, u32[]{:S(2)}, u32[]{:S(2)}) collective-permute-start(bf16[130,16,128]{2,1,0:T(8,128)(2,1)S(1)} %get-tuple-element.21.refs_0_), channel_id=1, source_target_pairs={{0,64},{64,128},{128,192},{192,0},{1,65},{65,129},{129,193},{193,1... | collective-permute-start | bytes 1597448 | tf_op jit(solution)/shard_map/ppermute | solution.py:426
  7.7 14.5 %collective-permute-start.1 = (bf16[130,16,128]{2,1,0:T(8,128)(2,1)S(1)}, bf16[130,16,128]{2,1,0:T(8,128)(2,1)S(1)}, u32[]{:S(2)}, u32[]{:S(2)}) collective-permute-start(bf16[130,16,128]{2,1,0:T(8,128)(2,1)S(1)} %get-tuple-element.21.refs_0_), channel_id=1, source_target_pairs={{0,192},{64,0},{128,64},{192,128},{1,193},{65,1},{129,65},{193,129... | collective-permute-start | bytes 1597448 | tf_op jit(solution)/shard_map/ppermute | solution.py:426
  9.2 20.8 %all-to-all-start = ((bf16[32,16,256]{2,1,0:T(8,128)(2,1)}), bf16[32,16,256]{2,1,0:T(8,128)(2,1)}, u32[]{:S(2)}, u32[]{:S(2)}) async-start(bf16[32,16,256]{2,1,0:T(8,128)(2,1)} %get-tuple-element.18), calls=%async_computation | async-start | bytes 524288 | tf_op jit(solution)/shard_map/all_to_all | solution.py:434
  20.4 11.2 %collective-permute-start.4 = (bf16[130,16,128]{2,1,0:T(8,128)(2,1)S(1)}, bf16[130,16,128]{2,1,0:T(8,128)(2,1)S(1)}, u32[]{:S(2)}, u32[]{:S(2)}) collective-permute-start(bf16[130,16,128]{2,1,0:T(8,128)(2,1)S(1)} %get-tuple-element.21.refs_0_), channel_id=1, source_target_pairs={{0,32},{32,0},{1,33},{33,1},{2,34},{34,2},{3,35},{35,3},{4,36},{36... | collective-permute-start | bytes 1597448 | tf_op jit(solution)/shard_map/ppermute | solution.py:429
  21.9 9.7 %collective-permute-start.5 = (bf16[130,16,128]{2,1,0:T(8,128)(2,1)S(1)}, bf16[130,16,128]{2,1,0:T(8,128)(2,1)S(1)}, u32[]{:S(2)}, u32[]{:S(2)}) collective-permute-start(bf16[130,16,128]{2,1,0:T(8,128)(2,1)S(1)} %collective-permute-done.near_ref.refs_2_), channel_id=1, source_target_pairs={{0,32},{32,0},{1,33},{33,1},{2,34},{34,2},{3,35},{35,3},{4,36},{36... | collective-permute-start | bytes 1597448 | tf_op jit(solution)/shard_map/ppermute | solution.py:429
  22.2 9.3 %collective-permute-start.6 = (bf16[130,16,128]{2,1,0:T(8,128)(2,1)S(1)}, bf16[130,16,128]{2,1,0:T(8,128)(2,1)S(1)}, u32[]{:S(2)}, u32[]{:S(2)}) collective-permute-start(bf16[130,16,128]{2,1,0:T(8,128)(2,1)S(1)} %collective-permute-done.1.far_ref.refs_4_), channel_id=1, source_target_pairs={{0,32},{32,0},{1,33},{33,1},{2,34},{34,2},{3,35},{35,3},{4,36},{36... | collective-permute-start | bytes 1597448 | tf_op jit(solution)/shard_map/ppermute | solution.py:429
  23.3 13.0 %collective-permute-start.3 = (bf16[66,16,128]{2,1,0:T(8,128)(2,1)}, bf16[66,16,128]{2,1,0:T(8,128)(2,1)S(1)}, u32[]{:S(2)}, u32[]{:S(2)}) collective-permute-start(bf16[66,16,128]{2,1,0:T(8,128)(2,1)} %get-tuple-element.23), channel_id=1, source_target_pairs={{0,192},{64,0},{128,64},{192,128},{1,193},{65,1},{129,65},{193,129... | collective-permute-start | bytes 811016 | tf_op jit(solution)/shard_map/ppermute | solution.py:426
  25.8 10.5 %collective-permute-start.2 = (bf16[64,16,128]{2,1,0:T(8,128)(2,1)}, bf16[64,16,128]{2,1,0:T(8,128)(2,1)}, u32[]{:S(2)}, u32[]{:S(2)}) collective-permute-start(bf16[64,16,128]{2,1,0:T(8,128)(2,1)} %get-tuple-element.22), channel_id=1, source_target_pairs={{0,64},{64,128},{128,192},{192,0},{1,65},{65,129},{129,193},{193,1... | collective-permute-start | bytes 786440 | tf_op jit(solution)/shard_map/ppermute | solution.py:426
  36.4 5.4 %collective-permute-start.8 = (bf16[66,16,128]{2,1,0:T(8,128)(2,1)S(1)}, bf16[66,16,128]{2,1,0:T(8,128)(2,1)S(1)}, u32[]{:S(2)}, u32[]{:S(2)}) collective-permute-start(bf16[66,16,128]{2,1,0:T(8,128)(2,1)S(1)} %collective-permute-done.3.refs_1_), channel_id=1, source_target_pairs={{0,32},{32,0},{1,33},{33,1},{2,34},{34,2},{3,35},{35,3},{4,36},{36... | collective-permute-start | bytes 811016 | tf_op jit(solution)/shard_map/ppermute | solution.py:429
  40.1 1.8 %collective-permute-start.7 = (bf16[64,16,128]{2,1,0:T(8,128)(2,1)}, bf16[64,16,128]{2,1,0:T(8,128)(2,1)S(1)}, u32[]{:S(2)}, u32[]{:S(2)}) collective-permute-start(bf16[64,16,128]{2,1,0:T(8,128)(2,1)} %collective-permute-done.2.refs_0_), channel_id=1, source_target_pairs={{0,32},{32,0},{1,33},{33,1},{2,34},{34,2},{3,35},{35,3},{4,36},{36... | collective-permute-start | bytes 786440 | tf_op jit(solution)/shard_map/ppermute | solution.py:429

commit v2 on v1

--- a/solution.py
+++ b/solution.py
@@ -114,23 +114,25 @@
     )(raw, taps, phase_error, chosen, start, bins, cross)
 
 
-def halves_kernel(near_ref, far_ref, first_ref, second_ref):
-    first_ref[...] = near_ref[:BLOCKS]
-    second_ref[...] = far_ref[BLOCKS:]
-
-
-def halves(near, far):
-    return pl.pallas_call(
-        halves_kernel,
-        out_shape=(
-            jax.ShapeDtypeStruct((BLOCKS, 2 * ROWS, 128), jnp.bfloat16),
-            jax.ShapeDtypeStruct((BLOCKS + 2, 2 * ROWS, 128), jnp.bfloat16),
-        ),
-        in_specs=[VMEM, VMEM],
-        out_specs=(VMEM, VMEM),
-        compiler_params=PARAMS,
-        name="halves",
-    )(near, far)
+def onward_kernel(core_ref, near_ref, far_ref, out_ref):
+    @pl.when(core_ref[0] == 0)
+    def _():
+        out_ref[...] = near_ref[...]
+
+    @pl.when(core_ref[0] != 0)
+    def _():
+        out_ref[...] = far_ref[...]
+
+
+def onward(core, near, far):
+    return pl.pallas_call(
+        onward_kernel,
+        out_shape=jax.ShapeDtypeStruct(near.shape, near.dtype),
+        in_specs=[SMEM, VMEM, VMEM],
+        out_specs=VMEM,
+        compiler_params=PARAMS,
+        name="onward",
+    )(core, near, far)
 
 
 def pieces(refs):
@@ -429,13 +431,16 @@
         return [block, tuple(lax.ppermute(x, "core", [(0, 1), (1, 0)]) for x in block)]
 
     near, far = back_by(own, 1), back_by(own, 3)
-    first, second = halves(near, far)
-    across = (back_by(first, 1), back_by(second, 3))
+    across = lax.ppermute(
+        onward(core.reshape(1), near, far),
+        ("y", "core"),
+        [(2 * at, 2 * ((at + 1) % 4)) for at in range(4)] + [(2 * at + 1, 2 * ((at + 3) % 4) + 1) for at in range(4)],
+    )
     known = lax.all_to_all(known, ("x", "z"), 0, 0, tiled=True)
     bins, phase = phases(groups, rates, known)
     before, kept_a, whole_a = image_parts(0, groups[:1], bins, phase, pair(own) + pair(near) + pair(far))
-    across = lax.optimization_barrier((*across, before))[:2]
-    parts, kept_b, whole_b = image_parts(EARLY, groups[:1], bins, phase, pair(*across), (before,))
+    across = lax.optimization_barrier((across, before))[0]
+    parts, kept_b, whole_b = image_parts(EARLY, groups[:1], bins, phase, pair(across), (before,))
     parts = lax.all_to_all(parts.reshape(PLANE, ROWS, PIX), ("x", "z"), 0, 0, tiled=True)
     image_tile, copies = total_image(parts)
     images = lax.all_to_all(copies, ("x", "z"), 0, 0, tiled=True)

time: 89.9 us -> 88.7 us (0.987)
    ppermute x0 -> x1, starting transfers between devices: none -> 2.62 us  [body(): lax.ppermute(onward(core.reshape(1), near, far), ('y', 'core'), [(2 * at,...]
    ppermute x4 -> x2, starting transfers between devices: 6.06 us -> 3.57 us  [back_by(): return lax.ppermute(x, 'y', [(at, (at + steps) % 4) for at in range(4)])]
    all_to_all x1, blocking collectives: 16 us -> 14.9 us  [body(): lax.all_to_all(parts.reshape(PLANE, ROWS, PIX), ('x', 'z'), 0, 0, tiled=T...]
    ppermute x5 -> x4, starting transfers between devices: 5.83 us -> 5.73 us  [pair(): lax.ppermute(x, 'core', [(0, 1), (1, 0)])]
  transfers between devices with their start and end apart: 10 -> 8, of which waited for: 2 -> 2; matrix products, arithmetic and copies ran while one was open for 0% -> 0% of each run, Pallas kernels for 8% -> 8%
where the time goes in v2:
time: 88.7 us; the launch traced here: 88.4 us
  blocking collectives  39.6 us (45%)
  starting transfers between devices  22.9 us (26%)
  Pallas kernels  16.5 us (19%)
  waiting for transfers between devices  5.81 us (7%)
  local copies, waits for them, and re-layouts  2.06 us (2%)
    all_to_all x1, blocking collectives, body(): lax.all_to_all(parts.reshape(PLANE, ROWS, PIX), ('x', 'z'), 0, 0, tiled=T...  14.9 us
    all_to_all x1, blocking collectives, body(): images = lax.all_to_all(copies, ('x', 'z'), 0, 0, tiled=True)  13.8 us
    all_to_all x1, starting transfers between devices, body(): known = lax.all_to_all(known, ('x', 'z'), 0, 0, tiled=True)  11 us
    all_to_all x1, blocking collectives, body(): grads = lax.all_to_all(grads, ('y', 'core'), 0, 0, tiled=True)  11 us
    pallas_call x2, Pallas kernels, image_parts(): pl.pallas_call(functools.partial(image_kernel, first, count, parts, last)...  8.63 us
    ppermute x4, starting transfers between devices, pair(): lax.ppermute(x, 'core', [(0, 1), (1, 0)])  5.73 us
    all_to_all x1, waiting for transfers between devices, body(): known = lax.all_to_all(known, ('x', 'z'), 0, 0, tiled=True)  4.03 us
    ppermute x2, starting transfers between devices, back_by(): return lax.ppermute(x, 'y', [(at, (at + steps) % 4) for at in range(4)])  3.57 us
  transfers between devices with their start and end apart: 8, of which 2 were waited for; matrix products, arithmetic and copies ran while one was open for 0% of the time, Pallas kernels for 8%

profile of v2, /device:TPU:1, one launch (start us, length us, event | category | flops | bytes accessed | tf_op | source)
XLA Modules:
  0.0 88.4 jit_solution(16755408903154285039)
XLA Ops:
  0.6 0.0 copy-start.5
  0.6 0.0 copy-start.1
  0.7 0.0 copy-start.2
  0.7 0.0 copy-start
  0.7 0.0 copy-start.3
  0.7 0.0 copy-start.4
  0.7 1.4 %reshape.16 = bf16[2,4,2,64,256]{4,3,2,1,0:T(8,128)(2,1)S(1)} reshape(bf16[2,4,2,16384]{3,2,1,0:T(2,128)(2,1)} %param.7) | data formatting | bytes 1048576 | tf_op jit(solution)/shard_map/reshape | solution.py:417
  2.1 0.4 copy.11
  2.5 0.1 reshape.17.raw_ref
  2.6 0.0 copy-done.5
  2.7 0.0 copy-done.1
  2.7 0.0 copy-done.2
  2.7 0.0 copy-done
  2.7 0.0 copy-done.3
  2.7 0.0 copy-done.4
  2.7 2.9 %compress.1 = (bf16[130,16,128]{2,1,0:T(8,128)(2,1)S(1)}, bf16[32,16,256]{2,1,0:T(8,128)(2,1)}) custom-call(bf16[1024,256]{1,0:T(8,128)(2,1)S(1)} %reshape.17.raw_ref, f32[2,1280]{1,0:T(2,128)S(1)} %pad.4.taps_ref, f32[2]{0:T(128)S(1)} %copy-done.4, s32[2,256]{1,0:T(2,128)S(1)} %bitcast.23, s32[2,256]{1,0:T(2,128)S(1)} %bitcast.24, s32[8,256]{1,0:T(8,128)S(1)} %bitcast.22, ...), custom_call_target="tpu_custom_call" | custom-call | tf_op jit(solution)/shard_map/compress/pallas_call | solution.py:100
  5.6 2.1 %collective-permute-start = (bf16[130,16,128]{2,1,0:T(8,128)(2,1)S(1)}, bf16[130,16,128]{2,1,0:T(8,128)(2,1)S(1)}, u32[]{:S(2)}, u32[]{:S(2)}) collective-permute-start(bf16[130,16,128]{2,1,0:T(8,128)(2,1)S(1)} %get-tuple-element.18.refs_0_), channel_id=1, source_target_pairs={{0,64},{64,128},{128,192},{192,0},{1,65},{65,129},{129,193},{193,1... | collective-permute-start | bytes 1597448 | tf_op jit(solution)/shard_map/ppermute | solution.py:428
  7.8 1.4 %collective-permute-start.1 = (bf16[130,16,128]{2,1,0:T(8,128)(2,1)S(1)}, bf16[130,16,128]{2,1,0:T(8,128)(2,1)S(1)}, u32[]{:S(2)}, u32[]{:S(2)}) collective-permute-start(bf16[130,16,128]{2,1,0:T(8,128)(2,1)S(1)} %get-tuple-element.18.refs_0_), channel_id=1, source_target_pairs={{0,192},{64,0},{128,64},{192,128},{1,193},{65,1},{129,65},{193,129... | collective-permute-start | bytes 1597448 | tf_op jit(solution)/shard_map/ppermute | solution.py:428
  9.2 11.0 %all-to-all-start = ((bf16[32,16,256]{2,1,0:T(8,128)(2,1)}), bf16[32,16,256]{2,1,0:T(8,128)(2,1)S(1)}, u32[]{:S(2)}, u32[]{:S(2)}) async-start(bf16[32,16,256]{2,1,0:T(8,128)(2,1)} %get-tuple-element.15), calls=%async_computation | async-start | bytes 524288 | tf_op jit(solution)/shard_map/all_to_all | solution.py:439
  20.2 1.5 %collective-permute-start.3 = (bf16[130,16,128]{2,1,0:T(8,128)(2,1)S(1)}, bf16[130,16,128]{2,1,0:T(8,128)(2,1)S(1)}, u32[]{:S(2)}, u32[]{:S(2)}) collective-permute-start(bf16[130,16,128]{2,1,0:T(8,128)(2,1)S(1)} %get-tuple-element.18.refs_0_), channel_id=1, source_target_pairs={{0,32},{32,0},{1,33},{33,1},{2,34},{34,2},{3,35},{35,3},{4,36},{36... | collective-permute-start | bytes 1597448 | tf_op jit(solution)/shard_map/ppermute | solution.py:431
  21.8 0.0 collective-permute-done.near_ref.refs_2_
  21.8 0.5 collective-permute-start.4
  22.3 0.0 collective-permute-done.1.far_ref.refs_4_
  22.3 0.1 collective-permute-start.5
  22.3 0.8 onward.1
  23.2 2.6 %collective-permute-start.2 = (bf16[130,16,128]{2,1,0:T(8,128)(2,1)}, bf16[130,16,128]{2,1,0:T(8,128)(2,1)}, u32[]{:S(2)}, u32[]{:S(2)}) collective-permute-start(bf16[130,16,128]{2,1,0:T(8,128)(2,1)} %onward.1), channel_id=1, source_target_pairs={{0,64},{64,128},{128,192},{192,0},{32,224},{96,32},{160,96},{224,1... | collective-permute-start | bytes 1597448 | tf_op jit(solution)/shard_map/ppermute | solution.py:434
  25.8 0.1 stack.35.group_ref
  25.9 4.0 %all-to-all-done.known_ref = bf16[32,16,256]{2,1,0:T(8,128)(2,1)S(1)} async-done(((bf16[32,16,256]{2,1,0:T(8,128)(2,1)}), bf16[32,16,256]{2,1,0:T(8,128)(2,1)S(1)}, u32[]{:S(2)}, u32[]{:S(2)}) %all-to-all-start) | async-done | bytes 262176 | tf_op jit(solution)/shard_map/all_to_all | solution.py:439
  29.9 1.1 %phases.1 = (s32[8,32,256]{2,1,0:T(8,128)S(1)}, f32[8,2,32,256]{3,2,1,0:T(8,128)S(1)}) custom-call(s32[8]{0:T(128)S(1)} %stack.35.group_ref, f32[8]{0:T(128)S(1)} %convert_multiply_fusion.rate_ref, bf16[32,16,256]{2,1,0:T(8,128)(2,1)S(1)} %all-to-all-done.known_ref), custom_call_target="tpu_custom_call" | custom-call | flops 1200000000 | bytes 1000000 | tf_op jit(solution)/shard_map/phases/pallas_call | solution.py:218
  31.0 0.0 collective-permute-done.3.refs_1_
  31.1 0.0 collective-permute-done.4.refs_3_
  31.1 0.0 collective-permute-done.5.refs_5_
  31.1 4.8 %image.2 = (f32[32,8,256]{2,1,0:T(8,128)S(1)}, bf16[32,6,16,256]{3,2,1,0:T(8,128)(2,1)S(1)}, s32[32,128]{1,0:T(8,128)S(1)}) custom-call(s32[1]{0:T(128)} %bitcast.group_ref, s32[8,32,256]{2,1,0:T(8,128)S(1)} %get-tuple-element.16.bins_ref, f32[8,2,32,256]{3,2,1,0:T(8,128)S(1)} %get-tuple-element.17.phase_ref, ...), custom_call_target="tpu_custom_call" | custom-call | flops 600000000 | bytes 1000000 | tf_op jit(solution)/shard_map/image/pallas_call | solution.py:311
  35.8 0.0 collective-permute-done.2.refs_0_
  35.9 3.7 %collective-permute-start.6 = (bf16[130,16,128]{2,1,0:T(8,128)(2,1)}, bf16[130,16,128]{2,1,0:T(8,128)(2,1)S(1)}, u32[]{:S(2)}, u32[]{:S(2)}) collective-permute-start(bf16[130,16,128]{2,1,0:T(8,128)(2,1)} %collective-permute-done.2.refs_0_), channel_id=1, source_target_pairs={{0,32},{32,0},{1,33},{33,1},{2,34},{34,2},{3,35},{35,3},{4,36},{36... | collective-permute-start | bytes 1597448 | tf_op jit(solution)/shard_map/ppermute | solution.py:431
  39.5 1.8 %collective-permute-done.6.refs_1_ = bf16[130,16,128]{2,1,0:T(8,128)(2,1)S(1)} collective-permute-done((bf16[130,16,128]{2,1,0:T(8,128)(2,1)}, bf16[130,16,128]{2,1,0:T(8,128)(2,1)S(1)}, u32[]{:S(2)}, u32[]{:S(2)}) %collective-permute-start.6) | collective-permute-done | bytes 532512 | tf_op jit(solution)/shard_map/ppermute | solution.py:431
  41.3 3.9 %image.3 = (bf16[256,256]{1,0:T(8,128)(2,1)S(1)}, bf16[32,2,16,256]{3,2,1,0:T(8,128)(2,1)S(1)}, s32[32,128]{1,0:T(8,128)S(1)}) custom-call(s32[1]{0:T(128)} %bitcast.group_ref, s32[8,32,256]{2,1,0:T(8,128)S(1)} %get-tuple-element.16.bins_ref, f32[8,2,32,256]{3,2,1,0:T(8,128)S(1)} %get-tuple-element.17.phase_ref, ...), custom_call_target="tpu_custom_call" | custom-call | flops 200000000 | bytes 1000000 | tf_op jit(solution)/shard_map/image/pallas_call | solution.py:311
  45.2 14.9 %all_to_all.20.parts_ref = bf16[32,8,256]{2,1,0:T(8,128)(2,1)S(1)} all-to-all(bf16[32,8,256]{2,1,0:T(8,128)(2,1)S(1)} %bitcast.21), channel_id=1, replica_groups=mesh['y'=4,'core'=2,'x'=4,'z'=8] {'x','z'}, dimensions={0} | all-to-all | bytes 262144 | tf_op jit(solution)/shard_map/all_to_all | solution.py:444
  60.0 0.7 total.1
  60.7 13.8 %all_to_all.21.image_ref = f32[32,8,256]{2,1,0:T(8,128)S(1)} all-to-all(f32[32,8,256]{2,1,0:T(8,128)S(1)} %get-tuple-element.25), channel_id=1, replica_groups=mesh['y'=4,'core'=2,'x'=4,'z'=8] {'x','z'}, dimensions={0} | all-to-all | bytes 524288 | tf_op jit(solution)/shard_map/all_to_all | solution.py:446
  74.5 2.4 %grad.1 = f32[8,1,128]{2,1,0:T(1,128)S(1)} custom-call(s32[8]{0:T(128)S(1)} %stack.35.group_ref, s32[32,128]{1,0:T(8,128)S(1)} %get-tuple-element.23.whole_a, s32[32,128]{1,0:T(8,128)S(1)} %get-tuple-element.24.whole_b, f32[32,8,256]{2,1,0:T(8,128)S(1)} %all_to_all.21.image_ref, bf16[32,6,16,256]{3,2,1,0:T(8,128)(2,1)S(1)} %get-tuple-element.26.kept_a, ...), custom_call_target="tpu_custom_call" | custom-call | tf_op jit(solution)/shard_map/grad/pallas_call | solution.py:400
  76.9 11.0 %all_to_all.22 = f32[8,1,128]{2,1,0:T(1,128)S(1)} all-to-all(f32[8,1,128]{2,1,0:T(1,128)S(1)} %grad.1), channel_id=1, replica_groups=mesh['y'=4,'core'=2,'x'=4,'z'=8] {'y','core'}, dimensions={0} | all-to-all | bytes 8192 | tf_op jit(solution)/shard_map/all_to_all | solution.py:448
  87.8 0.5 slice_reduce_fusion
  (2 shorter events, 0.0 us)
Async XLA Ops:
  0.6 2.0 %copy-start.5 = (f32[2,1024]{1,0:T(2,128)S(1)}, f32[2,1024]{1,0:T(2,128)}, u32[]{:S(2)}) copy-start(f32[2,1024]{1,0:T(2,128)} %param.8) | copy-start | bytes 24580
  0.6 2.0 %copy-start.1 = (s32[1,256,2]{1,2,0:T(2,128)S(1)}, s32[1,256,2]{1,2,0:T(2,128)}, u32[]{:S(2)}) copy-start(s32[1,256,2]{1,2,0:T(2,128)} %param.10) | copy-start | bytes 6148
  0.7 2.0 %copy-start.2 = (s32[1,256,2]{1,2,0:T(2,128)S(1)}, s32[1,256,2]{1,2,0:T(2,128)}, u32[]{:S(2)}) copy-start(s32[1,256,2]{1,2,0:T(2,128)} %param.11) | copy-start | bytes 6148
  0.7 2.0 %copy-start = (s32[1,8,256]{2,1,0:T(8,128)S(1)}, s32[1,8,256]{2,1,0:T(8,128)}, u32[]{:S(2)}) copy-start(s32[1,8,256]{2,1,0:T(8,128)} %param.12) | copy-start | bytes 24580
  0.7 2.0 %copy-start.3 = (f32[1,256]{1,0:T(1,128)S(1)}, f32[1,256]{1,0:T(1,128)}, u32[]{:S(2)}) copy-start(f32[1,256]{1,0:T(1,128)} %cross_ref.1) | copy-start | bytes 3076
  0.7 2.0 %copy-start.4 = (f32[2]{0:T(128)S(1)}, f32[2]{0:T(128)}, u32[]{:S(2)}) copy-start(f32[2]{0:T(128)} %error_ref.1) | copy-start | bytes 28
  5.6 16.2 %collective-permute-start = (bf16[130,16,128]{2,1,0:T(8,128)(2,1)S(1)}, bf16[130,16,128]{2,1,0:T(8,128)(2,1)S(1)}, u32[]{:S(2)}, u32[]{:S(2)}) collective-permute-start(bf16[130,16,128]{2,1,0:T(8,128)(2,1)S(1)} %get-tuple-element.18.refs_0_), channel_id=1, source_target_pairs={{0,64},{64,128},{128,192},{192,0},{1,65},{65,129},{129,193},{193,1... | collective-permute-start | bytes 1597448 | tf_op jit(solution)/shard_map/ppermute | solution.py:428
  7.8 14.5 %collective-permute-start.1 = (bf16[130,16,128]{2,1,0:T(8,128)(2,1)S(1)}, bf16[130,16,128]{2,1,0:T(8,128)(2,1)S(1)}, u32[]{:S(2)}, u32[]{:S(2)}) collective-permute-start(bf16[130,16,128]{2,1,0:T(8,128)(2,1)S(1)} %get-tuple-element.18.refs_0_), channel_id=1, source_target_pairs={{0,192},{64,0},{128,64},{192,128},{1,193},{65,1},{129,65},{193,129... | collective-permute-start | bytes 1597448 | tf_op jit(solution)/shard_map/ppermute | solution.py:428
  9.2 20.7 %all-to-all-start = ((bf16[32,16,256]{2,1,0:T(8,128)(2,1)}), bf16[32,16,256]{2,1,0:T(8,128)(2,1)S(1)}, u32[]{:S(2)}, u32[]{:S(2)}) async-start(bf16[32,16,256]{2,1,0:T(8,128)(2,1)} %get-tuple-element.15), calls=%async_computation | async-start | bytes 524288 | tf_op jit(solution)/shard_map/all_to_all | solution.py:439
  20.2 10.8 %collective-permute-start.3 = (bf16[130,16,128]{2,1,0:T(8,128)(2,1)S(1)}, bf16[130,16,128]{2,1,0:T(8,128)(2,1)S(1)}, u32[]{:S(2)}, u32[]{:S(2)}) collective-permute-start(bf16[130,16,128]{2,1,0:T(8,128)(2,1)S(1)} %get-tuple-element.18.refs_0_), channel_id=1, source_target_pairs={{0,32},{32,0},{1,33},{33,1},{2,34},{34,2},{3,35},{35,3},{4,36},{36... | collective-permute-start | bytes 1597448 | tf_op jit(solution)/shard_map/ppermute | solution.py:431
  21.8 9.3 %collective-permute-start.4 = (bf16[130,16,128]{2,1,0:T(8,128)(2,1)S(1)}, bf16[130,16,128]{2,1,0:T(8,128)(2,1)S(1)}, u32[]{:S(2)}, u32[]{:S(2)}) collective-permute-start(bf16[130,16,128]{2,1,0:T(8,128)(2,1)S(1)} %collective-permute-done.near_ref.refs_2_), channel_id=1, source_target_pairs={{0,32},{32,0},{1,33},{33,1},{2,34},{34,2},{3,35},{35,3},{4,36},{36... | collective-permute-start | bytes 1597448 | tf_op jit(solution)/shard_map/ppermute | solution.py:431
  22.3 8.8 %collective-permute-start.5 = (bf16[130,16,128]{2,1,0:T(8,128)(2,1)S(1)}, bf16[130,16,128]{2,1,0:T(8,128)(2,1)S(1)}, u32[]{:S(2)}, u32[]{:S(2)}) collective-permute-start(bf16[130,16,128]{2,1,0:T(8,128)(2,1)S(1)} %collective-permute-done.1.far_ref.refs_4_), channel_id=1, source_target_pairs={{0,32},{32,0},{1,33},{33,1},{2,34},{34,2},{3,35},{35,3},{4,36},{36... | collective-permute-start | bytes 1597448 | tf_op jit(solution)/shard_map/ppermute | solution.py:431
  23.2 12.7 %collective-permute-start.2 = (bf16[130,16,128]{2,1,0:T(8,128)(2,1)}, bf16[130,16,128]{2,1,0:T(8,128)(2,1)}, u32[]{:S(2)}, u32[]{:S(2)}) collective-permute-start(bf16[130,16,128]{2,1,0:T(8,128)(2,1)} %onward.1), channel_id=1, source_target_pairs={{0,64},{64,128},{128,192},{192,0},{32,224},{96,32},{160,96},{224,1... | collective-permute-start | bytes 1597448 | tf_op jit(solution)/shard_map/ppermute | solution.py:434
  35.9 5.4 %collective-permute-start.6 = (bf16[130,16,128]{2,1,0:T(8,128)(2,1)}, bf16[130,16,128]{2,1,0:T(8,128)(2,1)S(1)}, u32[]{:S(2)}, u32[]{:S(2)}) collective-permute-start(bf16[130,16,128]{2,1,0:T(8,128)(2,1)} %collective-permute-done.2.refs_0_), channel_id=1, source_target_pairs={{0,32},{32,0},{1,33},{33,1},{2,34},{34,2},{3,35},{35,3},{4,36},{36... | collective-permute-start | bytes 1597448 | tf_op jit(solution)/shard_map/ppermute | solution.py:431

commit v3 on v2

--- a/solution.py
+++ b/solution.py
@@ -133,6 +133,22 @@
         compiler_params=PARAMS,
         name="onward",
     )(core, near, far)
+
+
+def fetch_kernel(block_ref, out_ref):
+    out_ref[...] = block_ref[...]
+
+
+def fetched(block):
+    return pl.pallas_call(
+        fetch_kernel,
+        out_shape=jax.ShapeDtypeStruct(block.shape, block.dtype),
+        in_specs=[VMEM],
+        out_specs=VMEM,
+        compiler_params=PARAMS,
+        cost_estimate=pl.CostEstimate(flops=1_200_000_000, bytes_accessed=4_000_000, transcendentals=0),
+        name="fetch",
+    )(block)
 
 
 def pieces(refs):
@@ -440,7 +456,9 @@
     bins, phase = phases(groups, rates, known)
     before, kept_a, whole_a = image_parts(0, groups[:1], bins, phase, pair(own) + pair(near) + pair(far))
     across = lax.optimization_barrier((across, before))[0]
-    parts, kept_b, whole_b = image_parts(EARLY, groups[:1], bins, phase, pair(across), (before,))
+    pulses = pair(across)
+    pulses[0] = (fetched(across),)
+    parts, kept_b, whole_b = image_parts(EARLY, groups[:1], bins, phase, pulses, (before,))
     parts = lax.all_to_all(parts.reshape(PLANE, ROWS, PIX), ("x", "z"), 0, 0, tiled=True)
     image_tile, copies = total_image(parts)
     images = lax.all_to_all(copies, ("x", "z"), 0, 0, tiled=True)

time: 88.7 us -> 87.6 us (0.988)
  waiting for transfers between devices: 5.81 us -> 4.73 us
    ppermute x4, waiting for transfers between devices: 1.77 us -> 0.69 us  [pair(): lax.ppermute(x, 'core', [(0, 1), (1, 0)])]
    pallas_call x0 -> x1, Pallas kernels: none -> 1.08 us  [fetched(): pl.pallas_call(fetch_kernel, out_shape=jax.ShapeDtypeStruct(block.shape,...]
    pallas_call x2, Pallas kernels: 8.63 us -> 7.58 us  [image_parts(): pl.pallas_call(functools.partial(image_kernel, first, count, parts, last)...]
  transfers between devices with their start and end apart: 8 -> 8, of which waited for: 2 -> 2; matrix products, arithmetic and copies ran while one was open for 0% -> 0% of each run, Pallas kernels for 8% -> 9%
where the time goes in v3:
time: 87.6 us; the launch traced here: 87.3 us
  blocking collectives  39.6 us (45%)
  starting transfers between devices  23 us (26%)
  Pallas kernels  16.6 us (19%)
  waiting for transfers between devices  4.73 us (5%)
  local copies, waits for them, and re-layouts  2.06 us (2%)
    all_to_all x1, blocking collectives, body(): lax.all_to_all(parts.reshape(PLANE, ROWS, PIX), ('x', 'z'), 0, 0, tiled=T...  14.9 us
    all_to_all x1, blocking collectives, body(): images = lax.all_to_all(copies, ('x', 'z'), 0, 0, tiled=True)  13.8 us
    all_to_all x1, starting transfers between devices, body(): known = lax.all_to_all(known, ('x', 'z'), 0, 0, tiled=True)  11 us
    all_to_all x1, blocking collectives, body(): grads = lax.all_to_all(grads, ('y', 'core'), 0, 0, tiled=True)  11 us
    pallas_call x2, Pallas kernels, image_parts(): pl.pallas_call(functools.partial(image_kernel, first, count, parts, last)...  7.58 us
    ppermute x4, starting transfers between devices, pair(): lax.ppermute(x, 'core', [(0, 1), (1, 0)])  5.73 us
    all_to_all x1, waiting for transfers between devices, body(): known = lax.all_to_all(known, ('x', 'z'), 0, 0, tiled=True)  4.03 us
    ppermute x2, starting transfers between devices, back_by(): return lax.ppermute(x, 'y', [(at, (at + steps) % 4) for at in range(4)])  3.57 us
  transfers between devices with their start and end apart: 8, of which 2 were waited for; matrix products, arithmetic and copies ran while one was open for 0% of the time, Pallas kernels for 9%

profile of v3, /device:TPU:1, one launch (start us, length us, event | category | flops | bytes accessed | tf_op | source)
XLA Modules:
  0.0 87.3 jit_solution(12482667786434584153)
XLA Ops:
  0.6 0.0 copy-start.5
  0.6 0.0 copy-start.1
  0.7 0.0 copy-start.2
  0.7 0.0 copy-start
  0.7 0.0 copy-start.3
  0.7 0.0 copy-start.4
  0.7 1.4 %reshape.16 = bf16[2,4,2,64,256]{4,3,2,1,0:T(8,128)(2,1)S(1)} reshape(bf16[2,4,2,16384]{3,2,1,0:T(2,128)(2,1)} %param.7) | data formatting | bytes 1048576 | tf_op jit(solution)/shard_map/reshape | solution.py:433
  2.1 0.4 copy.11
  2.5 0.1 reshape.17.raw_ref
  2.6 0.0 copy-done.5
  2.7 0.0 copy-done.1
  2.7 0.0 copy-done.2
  2.7 0.0 copy-done
  2.7 0.0 copy-done.3
  2.7 0.0 copy-done.4
  2.7 2.9 %compress.1 = (bf16[130,16,128]{2,1,0:T(8,128)(2,1)S(1)}, bf16[32,16,256]{2,1,0:T(8,128)(2,1)}) custom-call(bf16[1024,256]{1,0:T(8,128)(2,1)S(1)} %reshape.17.raw_ref, f32[2,1280]{1,0:T(2,128)S(1)} %pad.4.taps_ref, f32[2]{0:T(128)S(1)} %copy-done.4, s32[2,256]{1,0:T(2,128)S(1)} %bitcast.23, s32[2,256]{1,0:T(2,128)S(1)} %bitcast.24, s32[8,256]{1,0:T(8,128)S(1)} %bitcast.22, ...), custom_call_target="tpu_custom_call" | custom-call | tf_op jit(solution)/shard_map/compress/pallas_call | solution.py:100
  5.6 2.1 %collective-permute-start = (bf16[130,16,128]{2,1,0:T(8,128)(2,1)S(1)}, bf16[130,16,128]{2,1,0:T(8,128)(2,1)S(1)}, u32[]{:S(2)}, u32[]{:S(2)}) collective-permute-start(bf16[130,16,128]{2,1,0:T(8,128)(2,1)S(1)} %get-tuple-element.18.refs_0_), channel_id=1, source_target_pairs={{0,64},{64,128},{128,192},{192,0},{1,65},{65,129},{129,193},{193,1... | collective-permute-start | bytes 1597448 | tf_op jit(solution)/shard_map/ppermute | solution.py:444
  7.8 1.4 %collective-permute-start.1 = (bf16[130,16,128]{2,1,0:T(8,128)(2,1)S(1)}, bf16[130,16,128]{2,1,0:T(8,128)(2,1)S(1)}, u32[]{:S(2)}, u32[]{:S(2)}) collective-permute-start(bf16[130,16,128]{2,1,0:T(8,128)(2,1)S(1)} %get-tuple-element.18.refs_0_), channel_id=1, source_target_pairs={{0,192},{64,0},{128,64},{192,128},{1,193},{65,1},{129,65},{193,129... | collective-permute-start | bytes 1597448 | tf_op jit(solution)/shard_map/ppermute | solution.py:444
  9.2 11.0 %all-to-all-start = ((bf16[32,16,256]{2,1,0:T(8,128)(2,1)}), bf16[32,16,256]{2,1,0:T(8,128)(2,1)S(1)}, u32[]{:S(2)}, u32[]{:S(2)}) async-start(bf16[32,16,256]{2,1,0:T(8,128)(2,1)} %get-tuple-element.15), calls=%async_computation | async-start | bytes 524288 | tf_op jit(solution)/shard_map/all_to_all | solution.py:455
  20.2 1.5 %collective-permute-start.3 = (bf16[130,16,128]{2,1,0:T(8,128)(2,1)S(1)}, bf16[130,16,128]{2,1,0:T(8,128)(2,1)S(1)}, u32[]{:S(2)}, u32[]{:S(2)}) collective-permute-start(bf16[130,16,128]{2,1,0:T(8,128)(2,1)S(1)} %get-tuple-element.18.refs_0_), channel_id=1, source_target_pairs={{0,32},{32,0},{1,33},{33,1},{2,34},{34,2},{3,35},{35,3},{4,36},{36... | collective-permute-start | bytes 1597448 | tf_op jit(solution)/shard_map/ppermute | solution.py:447
  21.8 0.0 collective-permute-done.near_ref.refs_2_
  21.8 0.5 collective-permute-start.4
  22.3 0.0 collective-permute-done.1.far_ref.refs_4_
  22.3 0.1 collective-permute-start.5
  22.3 0.8 onward.1
  23.2 2.6 %collective-permute-start.2 = (bf16[130,16,128]{2,1,0:T(8,128)(2,1)}, bf16[130,16,128]{2,1,0:T(8,128)(2,1)}, u32[]{:S(2)}, u32[]{:S(2)}) collective-permute-start(bf16[130,16,128]{2,1,0:T(8,128)(2,1)} %onward.1), channel_id=1, source_target_pairs={{0,64},{64,128},{128,192},{192,0},{32,224},{96,32},{160,96},{224,1... | collective-permute-start | bytes 1597448 | tf_op jit(solution)/shard_map/ppermute | solution.py:450
  25.8 0.1 stack.35.group_ref
  25.9 4.0 %all-to-all-done.known_ref = bf16[32,16,256]{2,1,0:T(8,128)(2,1)S(1)} async-done(((bf16[32,16,256]{2,1,0:T(8,128)(2,1)}), bf16[32,16,256]{2,1,0:T(8,128)(2,1)S(1)}, u32[]{:S(2)}, u32[]{:S(2)}) %all-to-all-start) | async-done | bytes 262176 | tf_op jit(solution)/shard_map/all_to_all | solution.py:455
  29.9 1.1 %phases.1 = (s32[8,32,256]{2,1,0:T(8,128)S(1)}, f32[8,2,32,256]{3,2,1,0:T(8,128)S(1)}) custom-call(s32[8]{0:T(128)S(1)} %stack.35.group_ref, f32[8]{0:T(128)S(1)} %convert_multiply_fusion.rate_ref, bf16[32,16,256]{2,1,0:T(8,128)(2,1)S(1)} %all-to-all-done.known_ref), custom_call_target="tpu_custom_call" | custom-call | flops 1200000000 | bytes 1000000 | tf_op jit(solution)/shard_map/phases/pallas_call | solution.py:234
  31.0 0.0 collective-permute-done.3.refs_1_
  31.1 0.0 collective-permute-done.4.refs_3_
  31.1 0.0 collective-permute-done.5.refs_5_
  31.1 4.8 %image.2 = (f32[32,8,256]{2,1,0:T(8,128)S(1)}, bf16[32,6,16,256]{3,2,1,0:T(8,128)(2,1)S(1)}, s32[32,128]{1,0:T(8,128)S(1)}) custom-call(s32[1]{0:T(128)} %bitcast.group_ref, s32[8,32,256]{2,1,0:T(8,128)S(1)} %get-tuple-element.16.bins_ref, f32[8,2,32,256]{3,2,1,0:T(8,128)S(1)} %get-tuple-element.17.phase_ref, ...), custom_call_target="tpu_custom_call" | custom-call | flops 600000000 | bytes 1000000 | tf_op jit(solution)/shard_map/image/pallas_call | solution.py:327
  35.8 0.0 collective-permute-done.2.block_ref
  35.9 3.7 %collective-permute-start.6 = (bf16[130,16,128]{2,1,0:T(8,128)(2,1)}, bf16[130,16,128]{2,1,0:T(8,128)(2,1)S(1)}, u32[]{:S(2)}, u32[]{:S(2)}) collective-permute-start(bf16[130,16,128]{2,1,0:T(8,128)(2,1)} %collective-permute-done.2.block_ref), channel_id=1, source_target_pairs={{0,32},{32,0},{1,33},{33,1},{2,34},{34,2},{3,35},{35,3},{4,36},{36... | collective-permute-start | bytes 1597448 | tf_op jit(solution)/shard_map/ppermute | solution.py:447
  39.5 1.1 %fetch.1.refs_0_ = bf16[130,16,128]{2,1,0:T(8,128)(2,1)S(1)} custom-call(bf16[130,16,128]{2,1,0:T(8,128)(2,1)} %collective-permute-done.2.block_ref), custom_call_target="tpu_custom_call" | custom-call | flops 1200000000 | bytes 4000000 | tf_op jit(solution)/shard_map/fetch/pallas_call | solution.py:143
  40.6 0.7 collective-permute-done.6.refs_1_
  41.3 2.8 %image.3 = (bf16[256,256]{1,0:T(8,128)(2,1)S(1)}, bf16[32,2,16,256]{3,2,1,0:T(8,128)(2,1)S(1)}, s32[32,128]{1,0:T(8,128)S(1)}) custom-call(s32[1]{0:T(128)} %bitcast.group_ref, s32[8,32,256]{2,1,0:T(8,128)S(1)} %get-tuple-element.16.bins_ref, f32[8,2,32,256]{3,2,1,0:T(8,128)S(1)} %get-tuple-element.17.phase_ref, bf16[130,16,128]{2,1,0:T(8,128)(2,1)S(1)} %fetch.1.refs_0_, ...), custom_call_target="tpu_custom_call" | custom-call | flops 200000000 | bytes 1000000 | tf_op jit(solution)/shard_map/image/pallas_call | solution.py:327
  44.1 14.9 %all_to_all.20.parts_ref = bf16[32,8,256]{2,1,0:T(8,128)(2,1)S(1)} all-to-all(bf16[32,8,256]{2,1,0:T(8,128)(2,1)S(1)} %bitcast.21), channel_id=1, replica_groups=mesh['y'=4,'core'=2,'x'=4,'z'=8] {'x','z'}, dimensions={0} | all-to-all | bytes 262144 | tf_op jit(solution)/shard_map/all_to_all | solution.py:462
  59.0 0.7 total.1
  59.6 13.8 %all_to_all.21.image_ref = f32[32,8,256]{2,1,0:T(8,128)S(1)} all-to-all(f32[32,8,256]{2,1,0:T(8,128)S(1)} %get-tuple-element.25), channel_id=1, replica_groups=mesh['y'=4,'core'=2,'x'=4,'z'=8] {'x','z'}, dimensions={0} | all-to-all | bytes 524288 | tf_op jit(solution)/shard_map/all_to_all | solution.py:464
  73.4 2.4 %grad.1 = f32[8,1,128]{2,1,0:T(1,128)S(1)} custom-call(s32[8]{0:T(128)S(1)} %stack.35.group_ref, s32[32,128]{1,0:T(8,128)S(1)} %get-tuple-element.23.whole_a, s32[32,128]{1,0:T(8,128)S(1)} %get-tuple-element.24.whole_b, f32[32,8,256]{2,1,0:T(8,128)S(1)} %all_to_all.21.image_ref, bf16[32,6,16,256]{3,2,1,0:T(8,128)(2,1)S(1)} %get-tuple-element.26.kept_a, ...), custom_call_target="tpu_custom_call" | custom-call | tf_op jit(solution)/shard_map/grad/pallas_call | solution.py:416
  75.8 11.0 %all_to_all.22 = f32[8,1,128]{2,1,0:T(1,128)S(1)} all-to-all(f32[8,1,128]{2,1,0:T(1,128)S(1)} %grad.1), channel_id=1, replica_groups=mesh['y'=4,'core'=2,'x'=4,'z'=8] {'y','core'}, dimensions={0} | all-to-all | bytes 8192 | tf_op jit(solution)/shard_map/all_to_all | solution.py:466
  86.8 0.5 slice_reduce_fusion
  (2 shorter events, 0.0 us)
Async XLA Ops:
  0.6 2.0 %copy-start.5 = (f32[2,1024]{1,0:T(2,128)S(1)}, f32[2,1024]{1,0:T(2,128)}, u32[]{:S(2)}) copy-start(f32[2,1024]{1,0:T(2,128)} %param.8) | copy-start | bytes 24580
  0.6 2.0 %copy-start.1 = (s32[1,256,2]{1,2,0:T(2,128)S(1)}, s32[1,256,2]{1,2,0:T(2,128)}, u32[]{:S(2)}) copy-start(s32[1,256,2]{1,2,0:T(2,128)} %param.10) | copy-start | bytes 6148
  0.7 2.0 %copy-start.2 = (s32[1,256,2]{1,2,0:T(2,128)S(1)}, s32[1,256,2]{1,2,0:T(2,128)}, u32[]{:S(2)}) copy-start(s32[1,256,2]{1,2,0:T(2,128)} %param.11) | copy-start | bytes 6148
  0.7 2.0 %copy-start = (s32[1,8,256]{2,1,0:T(8,128)S(1)}, s32[1,8,256]{2,1,0:T(8,128)}, u32[]{:S(2)}) copy-start(s32[1,8,256]{2,1,0:T(8,128)} %param.12) | copy-start | bytes 24580
  0.7 2.0 %copy-start.3 = (f32[1,256]{1,0:T(1,128)S(1)}, f32[1,256]{1,0:T(1,128)}, u32[]{:S(2)}) copy-start(f32[1,256]{1,0:T(1,128)} %cross_ref.1) | copy-start | bytes 3076
  0.7 2.0 %copy-start.4 = (f32[2]{0:T(128)S(1)}, f32[2]{0:T(128)}, u32[]{:S(2)}) copy-start(f32[2]{0:T(128)} %error_ref.1) | copy-start | bytes 28
  5.6 16.2 %collective-permute-start = (bf16[130,16,128]{2,1,0:T(8,128)(2,1)S(1)}, bf16[130,16,128]{2,1,0:T(8,128)(2,1)S(1)}, u32[]{:S(2)}, u32[]{:S(2)}) collective-permute-start(bf16[130,16,128]{2,1,0:T(8,128)(2,1)S(1)} %get-tuple-element.18.refs_0_), channel_id=1, source_target_pairs={{0,64},{64,128},{128,192},{192,0},{1,65},{65,129},{129,193},{193,1... | collective-permute-start | bytes 1597448 | tf_op jit(solution)/shard_map/ppermute | solution.py:444
  7.8 14.5 %collective-permute-start.1 = (bf16[130,16,128]{2,1,0:T(8,128)(2,1)S(1)}, bf16[130,16,128]{2,1,0:T(8,128)(2,1)S(1)}, u32[]{:S(2)}, u32[]{:S(2)}) collective-permute-start(bf16[130,16,128]{2,1,0:T(8,128)(2,1)S(1)} %get-tuple-element.18.refs_0_), channel_id=1, source_target_pairs={{0,192},{64,0},{128,64},{192,128},{1,193},{65,1},{129,65},{193,129... | collective-permute-start | bytes 1597448 | tf_op jit(solution)/shard_map/ppermute | solution.py:444
  9.2 20.7 %all-to-all-start = ((bf16[32,16,256]{2,1,0:T(8,128)(2,1)}), bf16[32,16,256]{2,1,0:T(8,128)(2,1)S(1)}, u32[]{:S(2)}, u32[]{:S(2)}) async-start(bf16[32,16,256]{2,1,0:T(8,128)(2,1)} %get-tuple-element.15), calls=%async_computation | async-start | bytes 524288 | tf_op jit(solution)/shard_map/all_to_all | solution.py:455
  20.2 10.8 %collective-permute-start.3 = (bf16[130,16,128]{2,1,0:T(8,128)(2,1)S(1)}, bf16[130,16,128]{2,1,0:T(8,128)(2,1)S(1)}, u32[]{:S(2)}, u32[]{:S(2)}) collective-permute-start(bf16[130,16,128]{2,1,0:T(8,128)(2,1)S(1)} %get-tuple-element.18.refs_0_), channel_id=1, source_target_pairs={{0,32},{32,0},{1,33},{33,1},{2,34},{34,2},{3,35},{35,3},{4,36},{36... | collective-permute-start | bytes 1597448 | tf_op jit(solution)/shard_map/ppermute | solution.py:447
  21.8 9.3 %collective-permute-start.4 = (bf16[130,16,128]{2,1,0:T(8,128)(2,1)S(1)}, bf16[130,16,128]{2,1,0:T(8,128)(2,1)S(1)}, u32[]{:S(2)}, u32[]{:S(2)}) collective-permute-start(bf16[130,16,128]{2,1,0:T(8,128)(2,1)S(1)} %collective-permute-done.near_ref.refs_2_), channel_id=1, source_target_pairs={{0,32},{32,0},{1,33},{33,1},{2,34},{34,2},{3,35},{35,3},{4,36},{36... | collective-permute-start | bytes 1597448 | tf_op jit(solution)/shard_map/ppermute | solution.py:447
  22.3 8.8 %collective-permute-start.5 = (bf16[130,16,128]{2,1,0:T(8,128)(2,1)S(1)}, bf16[130,16,128]{2,1,0:T(8,128)(2,1)S(1)}, u32[]{:S(2)}, u32[]{:S(2)}) collective-permute-start(bf16[130,16,128]{2,1,0:T(8,128)(2,1)S(1)} %collective-permute-done.1.far_ref.refs_4_), channel_id=1, source_target_pairs={{0,32},{32,0},{1,33},{33,1},{2,34},{34,2},{3,35},{35,3},{4,36},{36... | collective-permute-start | bytes 1597448 | tf_op jit(solution)/shard_map/ppermute | solution.py:447
  23.2 12.7 %collective-permute-start.2 = (bf16[130,16,128]{2,1,0:T(8,128)(2,1)}, bf16[130,16,128]{2,1,0:T(8,128)(2,1)}, u32[]{:S(2)}, u32[]{:S(2)}) collective-permute-start(bf16[130,16,128]{2,1,0:T(8,128)(2,1)} %onward.1), channel_id=1, source_target_pairs={{0,64},{64,128},{128,192},{192,0},{32,224},{96,32},{160,96},{224,1... | collective-permute-start | bytes 1597448 | tf_op jit(solution)/shard_map/ppermute | solution.py:450
  35.9 5.4 %collective-permute-start.6 = (bf16[130,16,128]{2,1,0:T(8,128)(2,1)}, bf16[130,16,128]{2,1,0:T(8,128)(2,1)S(1)}, u32[]{:S(2)}, u32[]{:S(2)}) collective-permute-start(bf16[130,16,128]{2,1,0:T(8,128)(2,1)} %collective-permute-done.2.block_ref), channel_id=1, source_target_pairs={{0,32},{32,0},{1,33},{33,1},{2,34},{34,2},{3,35},{35,3},{4,36},{36... | collective-permute-start | bytes 1597448 | tf_op jit(solution)/shard_map/ppermute | solution.py:447

commit v4 on v3

--- a/solution.py
+++ b/solution.py
@@ -43,13 +43,32 @@
 
 
 def compress_kernel(
-    raw_ref, taps_ref, error_ref, chosen_ref, start_ref, bins_ref, cross_ref, out_ref, known_ref, left_ref, odd_ref
+    raw_ref,
+    taps_ref,
+    error_hbm,
+    chosen_hbm,
+    start_hbm,
+    bins_hbm,
+    cross_hbm,
+    out_ref,
+    known_ref,
+    left_ref,
+    odd_ref,
+    error_ref,
+    chosen_ref,
+    start_ref,
+    bins_ref,
+    cross_ref,
+    sems,
 ):
-    known = [bins_ref[...].astype(jnp.float32) - 256.0] + three_parts(cross_ref[...])
-    known.append(jnp.zeros((5, PIX), jnp.float32))
-    known = jnp.concatenate(known, axis=0).astype(jnp.bfloat16)
-    for at in range(PLANE):
-        known_ref[at] = known
+    copies = [
+        pltpu.make_async_copy(source, target, sems.at[at])
+        for at, (source, target) in enumerate(
+            ((error_hbm, error_ref), (chosen_hbm, chosen_ref), (start_hbm, start_ref), (bins_hbm, bins_ref), (cross_hbm, cross_ref))
+        )
+    ]
+    for copy in copies:
+        copy.start()
 
     taps = taps_ref[...].astype(jnp.bfloat16).astype(jnp.float32)
     wide = []
@@ -87,6 +106,14 @@
             [done[:, :, :128], done[:, :, 128:]], axis=1
         ).astype(jnp.bfloat16)
 
+    for copy in copies:
+        copy.wait()
+    known = [bins_ref[...].astype(jnp.float32) - 256.0] + three_parts(cross_ref[...])
+    known.append(jnp.zeros((5, PIX), jnp.float32))
+    known = jnp.concatenate(known, axis=0).astype(jnp.bfloat16)
+    for at in range(PLANE):
+        known_ref[at] = known
+
     rows = [chosen_ref[...].astype(jnp.float32), start_ref[...].astype(jnp.float32)]
     for pulse in range(2):
         rows += three_parts(jnp.full((1, PIX), error_ref[pulse], jnp.float32))
@@ -103,11 +130,17 @@
             jax.ShapeDtypeStruct((2 * BLOCKS + 2, 2 * ROWS, 128), jnp.bfloat16),
             jax.ShapeDtypeStruct((PLANE, 16, PIX), jnp.bfloat16),
         ),
-        in_specs=[VMEM, VMEM, SMEM, VMEM, VMEM, VMEM, VMEM],
+        in_specs=[VMEM, VMEM] + [pl.BlockSpec(memory_space=pl.ANY)] * 5,
         out_specs=(VMEM, VMEM),
         scratch_shapes=[
             pltpu.VMEM((2 * (BLOCKS * ROWS + EDGE), BLOCK), jnp.bfloat16),
             pltpu.VMEM((2 * (BLOCKS * ROWS + EDGE), BLOCK), jnp.bfloat16),
+            pltpu.SMEM(phase_error.shape, jnp.float32),
+            pltpu.VMEM(chosen.shape, jnp.int32),
+            pltpu.VMEM(start.shape, jnp.int32),
+            pltpu.VMEM(bins.shape, jnp.int32),
+            pltpu.VMEM(cross.shape, jnp.float32),
+            pltpu.SemaphoreType.DMA((5,)),
         ],
         compiler_params=PARAMS,
         name="compress",
@@ -314,7 +347,7 @@
         sum_ref[tile] = jnp.concatenate(total, axis=1)
         return carry
 
-    lax.fori_loop(0, PLANE, step, 0, unroll=8 if last else 4)
+    lax.fori_loop(0, PLANE, step, 0, unroll=8)
     if last:
         part_ref[...] = sum_ref[...].reshape(PLANE * ROWS, PIX).astype(jnp.bfloat16)
 

time: 87.6 us -> 87.4 us (level)
  no operation moved by 1% of the time
where the time goes in v4:
time: 87.4 us; the launch traced here: 87.1 us
  blocking collectives  39.9 us (46%)
  starting transfers between devices  23.1 us (26%)
  Pallas kernels  15.9 us (18%)
  waiting for transfers between devices  4.72 us (5%)
  local copies, waits for them, and re-layouts  2.06 us (2%)
    all_to_all x1, blocking collectives, body(): lax.all_to_all(parts.reshape(PLANE, ROWS, PIX), ('x', 'z'), 0, 0, tiled=T...  15.1 us
    all_to_all x1, blocking collectives, body(): images = lax.all_to_all(copies, ('x', 'z'), 0, 0, tiled=True)  13.8 us
    all_to_all x1, blocking collectives, body(): grads = lax.all_to_all(grads, ('y', 'core'), 0, 0, tiled=True)  11 us
    all_to_all x1, starting transfers between devices, body(): known = lax.all_to_all(known, ('x', 'z'), 0, 0, tiled=True)  11 us
    pallas_call x2, Pallas kernels, image_parts(): pl.pallas_call(functools.partial(image_kernel, first, count, parts, last)...  7.28 us
    ppermute x4, starting transfers between devices, pair(): lax.ppermute(x, 'core', [(0, 1), (1, 0)])  5.66 us
    all_to_all x1, waiting for transfers between devices, body(): known = lax.all_to_all(known, ('x', 'z'), 0, 0, tiled=True)  4.03 us
    ppermute x2, starting transfers between devices, back_by(): return lax.ppermute(x, 'y', [(at, (at + steps) % 4) for at in range(4)])  3.74 us
  transfers between devices with their start and end apart: 8, of which 2 were waited for; matrix products, arithmetic and copies ran while one was open for 0% of the time, Pallas kernels for 9%

profile of v4, /device:TPU:1, one launch (start us, length us, event | category | flops | bytes accessed | tf_op | source)
XLA Modules:
  0.0 87.1 jit_solution(10642141342774798873)
XLA Ops:
  0.6 0.0 copy-start.5
  0.6 0.0 copy-start.1
  0.7 0.0 copy-start.2
  0.7 0.0 copy-start
  0.7 0.0 copy-start.3
  0.7 0.0 copy-start.4
  0.7 1.4 %reshape.16 = bf16[2,4,2,64,256]{4,3,2,1,0:T(8,128)(2,1)S(1)} reshape(bf16[2,4,2,16384]{3,2,1,0:T(2,128)(2,1)} %param.7) | data formatting | bytes 1048576 | tf_op jit(solution)/shard_map/reshape | solution.py:466
  2.1 0.4 copy.11
  2.5 0.1 reshape.17.raw_ref
  2.6 0.0 copy-done.5
  2.7 0.0 copy-done.1
  2.7 0.0 copy-done.2
  2.7 0.0 copy-done
  2.7 0.0 copy-done.3
  2.7 0.0 copy-done.4
  2.7 2.6 %compress.1 = (bf16[130,16,128]{2,1,0:T(8,128)(2,1)S(1)}, bf16[32,16,256]{2,1,0:T(8,128)(2,1)}) custom-call(bf16[1024,256]{1,0:T(8,128)(2,1)S(1)} %reshape.17.raw_ref, f32[2,1280]{1,0:T(2,128)S(1)} %pad.4.taps_ref, f32[2]{0:T(128)S(1)} %copy-done.4, s32[2,256]{1,0:T(2,128)S(1)} %bitcast.23, s32[2,256]{1,0:T(2,128)S(1)} %bitcast.24, s32[8,256]{1,0:T(8,128)S(1)} %bitcast.22, ...), custom_call_target="tpu_custom_call" | custom-call | tf_op jit(solution)/shard_map/compress/pallas_call | solution.py:127
  5.3 2.2 %collective-permute-start = (bf16[130,16,128]{2,1,0:T(8,128)(2,1)S(1)}, bf16[130,16,128]{2,1,0:T(8,128)(2,1)S(1)}, u32[]{:S(2)}, u32[]{:S(2)}) collective-permute-start(bf16[130,16,128]{2,1,0:T(8,128)(2,1)S(1)} %get-tuple-element.18.refs_0_), channel_id=1, source_target_pairs={{0,64},{64,128},{128,192},{192,0},{1,65},{65,129},{129,193},{193,1... | collective-permute-start | bytes 1597448 | tf_op jit(solution)/shard_map/ppermute | solution.py:477
  7.5 1.5 %collective-permute-start.1 = (bf16[130,16,128]{2,1,0:T(8,128)(2,1)S(1)}, bf16[130,16,128]{2,1,0:T(8,128)(2,1)S(1)}, u32[]{:S(2)}, u32[]{:S(2)}) collective-permute-start(bf16[130,16,128]{2,1,0:T(8,128)(2,1)S(1)} %get-tuple-element.18.refs_0_), channel_id=1, source_target_pairs={{0,192},{64,0},{128,64},{192,128},{1,193},{65,1},{129,65},{193,129... | collective-permute-start | bytes 1597448 | tf_op jit(solution)/shard_map/ppermute | solution.py:477
  9.0 11.0 %all-to-all-start = ((bf16[32,16,256]{2,1,0:T(8,128)(2,1)}), bf16[32,16,256]{2,1,0:T(8,128)(2,1)S(1)}, u32[]{:S(2)}, u32[]{:S(2)}) async-start(bf16[32,16,256]{2,1,0:T(8,128)(2,1)} %get-tuple-element.15), calls=%async_computation | async-start | bytes 524288 | tf_op jit(solution)/shard_map/all_to_all | solution.py:488
  20.1 1.5 %collective-permute-start.3 = (bf16[130,16,128]{2,1,0:T(8,128)(2,1)S(1)}, bf16[130,16,128]{2,1,0:T(8,128)(2,1)S(1)}, u32[]{:S(2)}, u32[]{:S(2)}) collective-permute-start(bf16[130,16,128]{2,1,0:T(8,128)(2,1)S(1)} %get-tuple-element.18.refs_0_), channel_id=1, source_target_pairs={{0,32},{32,0},{1,33},{33,1},{2,34},{34,2},{3,35},{35,3},{4,36},{36... | collective-permute-start | bytes 1597448 | tf_op jit(solution)/shard_map/ppermute | solution.py:480
  21.5 0.0 collective-permute-done.near_ref.refs_2_
  21.5 0.5 collective-permute-start.4
  22.0 0.0 collective-permute-done.1.far_ref.refs_4_
  22.0 0.0 collective-permute-start.5
  22.0 0.8 onward.1
  22.9 2.7 %collective-permute-start.2 = (bf16[130,16,128]{2,1,0:T(8,128)(2,1)}, bf16[130,16,128]{2,1,0:T(8,128)(2,1)}, u32[]{:S(2)}, u32[]{:S(2)}) collective-permute-start(bf16[130,16,128]{2,1,0:T(8,128)(2,1)} %onward.1), channel_id=1, source_target_pairs={{0,64},{64,128},{128,192},{192,0},{32,224},{96,32},{160,96},{224,1... | collective-permute-start | bytes 1597448 | tf_op jit(solution)/shard_map/ppermute | solution.py:483
  25.6 0.1 stack.35.group_ref
  25.7 4.0 %all-to-all-done.known_ref = bf16[32,16,256]{2,1,0:T(8,128)(2,1)S(1)} async-done(((bf16[32,16,256]{2,1,0:T(8,128)(2,1)}), bf16[32,16,256]{2,1,0:T(8,128)(2,1)S(1)}, u32[]{:S(2)}, u32[]{:S(2)}) %all-to-all-start) | async-done | bytes 262176 | tf_op jit(solution)/shard_map/all_to_all | solution.py:488
  29.7 1.1 %phases.1 = (s32[8,32,256]{2,1,0:T(8,128)S(1)}, f32[8,2,32,256]{3,2,1,0:T(8,128)S(1)}) custom-call(s32[8]{0:T(128)S(1)} %stack.35.group_ref, f32[8]{0:T(128)S(1)} %convert_multiply_fusion.rate_ref, bf16[32,16,256]{2,1,0:T(8,128)(2,1)S(1)} %all-to-all-done.known_ref), custom_call_target="tpu_custom_call" | custom-call | flops 1200000000 | bytes 1000000 | tf_op jit(solution)/shard_map/phases/pallas_call | solution.py:267
  30.9 0.0 collective-permute-done.3.refs_1_
  30.9 0.0 collective-permute-done.4.refs_3_
  30.9 0.0 collective-permute-done.5.refs_5_
  30.9 4.5 %image.2 = (f32[32,8,256]{2,1,0:T(8,128)S(1)}, bf16[32,6,16,256]{3,2,1,0:T(8,128)(2,1)S(1)}, s32[32,128]{1,0:T(8,128)S(1)}) custom-call(s32[1]{0:T(128)} %bitcast.group_ref, s32[8,32,256]{2,1,0:T(8,128)S(1)} %get-tuple-element.16.bins_ref, f32[8,2,32,256]{3,2,1,0:T(8,128)S(1)} %get-tuple-element.17.phase_ref, ...), custom_call_target="tpu_custom_call" | custom-call | flops 600000000 | bytes 1000000 | tf_op jit(solution)/shard_map/image/pallas_call | solution.py:360
  35.4 0.0 collective-permute-done.2.block_ref
  35.4 3.7 %collective-permute-start.6 = (bf16[130,16,128]{2,1,0:T(8,128)(2,1)}, bf16[130,16,128]{2,1,0:T(8,128)(2,1)S(1)}, u32[]{:S(2)}, u32[]{:S(2)}) collective-permute-start(bf16[130,16,128]{2,1,0:T(8,128)(2,1)} %collective-permute-done.2.block_ref), channel_id=1, source_target_pairs={{0,32},{32,0},{1,33},{33,1},{2,34},{34,2},{3,35},{35,3},{4,36},{36... | collective-permute-start | bytes 1597448 | tf_op jit(solution)/shard_map/ppermute | solution.py:480
  39.1 1.1 %fetch.1.refs_0_ = bf16[130,16,128]{2,1,0:T(8,128)(2,1)S(1)} custom-call(bf16[130,16,128]{2,1,0:T(8,128)(2,1)} %collective-permute-done.2.block_ref), custom_call_target="tpu_custom_call" | custom-call | flops 1200000000 | bytes 4000000 | tf_op jit(solution)/shard_map/fetch/pallas_call | solution.py:176
  40.1 0.7 collective-permute-done.6.refs_1_
  40.8 2.8 %image.3 = (bf16[256,256]{1,0:T(8,128)(2,1)S(1)}, bf16[32,2,16,256]{3,2,1,0:T(8,128)(2,1)S(1)}, s32[32,128]{1,0:T(8,128)S(1)}) custom-call(s32[1]{0:T(128)} %bitcast.group_ref, s32[8,32,256]{2,1,0:T(8,128)S(1)} %get-tuple-element.16.bins_ref, f32[8,2,32,256]{3,2,1,0:T(8,128)S(1)} %get-tuple-element.17.phase_ref, bf16[130,16,128]{2,1,0:T(8,128)(2,1)S(1)} %fetch.1.refs_0_, ...), custom_call_target="tpu_custom_call" | custom-call | flops 200000000 | bytes 1000000 | tf_op jit(solution)/shard_map/image/pallas_call | solution.py:360
  43.6 15.1 %all_to_all.20.parts_ref = bf16[32,8,256]{2,1,0:T(8,128)(2,1)S(1)} all-to-all(bf16[32,8,256]{2,1,0:T(8,128)(2,1)S(1)} %bitcast.21), channel_id=1, replica_groups=mesh['y'=4,'core'=2,'x'=4,'z'=8] {'x','z'}, dimensions={0} | all-to-all | bytes 262144 | tf_op jit(solution)/shard_map/all_to_all | solution.py:495
  58.7 0.7 total.1
  59.4 13.8 %all_to_all.21.image_ref = f32[32,8,256]{2,1,0:T(8,128)S(1)} all-to-all(f32[32,8,256]{2,1,0:T(8,128)S(1)} %get-tuple-element.25), channel_id=1, replica_groups=mesh['y'=4,'core'=2,'x'=4,'z'=8] {'x','z'}, dimensions={0} | all-to-all | bytes 524288 | tf_op jit(solution)/shard_map/all_to_all | solution.py:497
  73.2 2.4 %grad.1 = f32[8,1,128]{2,1,0:T(1,128)S(1)} custom-call(s32[8]{0:T(128)S(1)} %stack.35.group_ref, s32[32,128]{1,0:T(8,128)S(1)} %get-tuple-element.23.whole_a, s32[32,128]{1,0:T(8,128)S(1)} %get-tuple-element.24.whole_b, f32[32,8,256]{2,1,0:T(8,128)S(1)} %all_to_all.21.image_ref, bf16[32,6,16,256]{3,2,1,0:T(8,128)(2,1)S(1)} %get-tuple-element.26.kept_a, ...), custom_call_target="tpu_custom_call" | custom-call | tf_op jit(solution)/shard_map/grad/pallas_call | solution.py:449
  75.5 11.0 %all_to_all.22 = f32[8,1,128]{2,1,0:T(1,128)S(1)} all-to-all(f32[8,1,128]{2,1,0:T(1,128)S(1)} %grad.1), channel_id=1, replica_groups=mesh['y'=4,'core'=2,'x'=4,'z'=8] {'y','core'}, dimensions={0} | all-to-all | bytes 8192 | tf_op jit(solution)/shard_map/all_to_all | solution.py:499
  86.6 0.5 slice_reduce_fusion
  (2 shorter events, 0.0 us)
Async XLA Ops:
  0.6 2.0 %copy-start.5 = (f32[2,1024]{1,0:T(2,128)S(1)}, f32[2,1024]{1,0:T(2,128)}, u32[]{:S(2)}) copy-start(f32[2,1024]{1,0:T(2,128)} %param.8) | copy-start | bytes 24580
  0.6 2.0 %copy-start.1 = (s32[1,256,2]{1,2,0:T(2,128)S(1)}, s32[1,256,2]{1,2,0:T(2,128)}, u32[]{:S(2)}) copy-start(s32[1,256,2]{1,2,0:T(2,128)} %param.10) | copy-start | bytes 6148
  0.7 2.0 %copy-start.2 = (s32[1,256,2]{1,2,0:T(2,128)S(1)}, s32[1,256,2]{1,2,0:T(2,128)}, u32[]{:S(2)}) copy-start(s32[1,256,2]{1,2,0:T(2,128)} %param.11) | copy-start | bytes 6148
  0.7 2.0 %copy-start = (s32[1,8,256]{2,1,0:T(8,128)S(1)}, s32[1,8,256]{2,1,0:T(8,128)}, u32[]{:S(2)}) copy-start(s32[1,8,256]{2,1,0:T(8,128)} %param.12) | copy-start | bytes 24580
  0.7 2.0 %copy-start.3 = (f32[1,256]{1,0:T(1,128)S(1)}, f32[1,256]{1,0:T(1,128)}, u32[]{:S(2)}) copy-start(f32[1,256]{1,0:T(1,128)} %cross_hbm.1) | copy-start | bytes 3076
  0.7 2.0 %copy-start.4 = (f32[2]{0:T(128)S(1)}, f32[2]{0:T(128)}, u32[]{:S(2)}) copy-start(f32[2]{0:T(128)} %error_hbm.1) | copy-start | bytes 28
  5.3 16.2 %collective-permute-start = (bf16[130,16,128]{2,1,0:T(8,128)(2,1)S(1)}, bf16[130,16,128]{2,1,0:T(8,128)(2,1)S(1)}, u32[]{:S(2)}, u32[]{:S(2)}) collective-permute-start(bf16[130,16,128]{2,1,0:T(8,128)(2,1)S(1)} %get-tuple-element.18.refs_0_), channel_id=1, source_target_pairs={{0,64},{64,128},{128,192},{192,0},{1,65},{65,129},{129,193},{193,1... | collective-permute-start | bytes 1597448 | tf_op jit(solution)/shard_map/ppermute | solution.py:477
  7.5 14.5 %collective-permute-start.1 = (bf16[130,16,128]{2,1,0:T(8,128)(2,1)S(1)}, bf16[130,16,128]{2,1,0:T(8,128)(2,1)S(1)}, u32[]{:S(2)}, u32[]{:S(2)}) collective-permute-start(bf16[130,16,128]{2,1,0:T(8,128)(2,1)S(1)} %get-tuple-element.18.refs_0_), channel_id=1, source_target_pairs={{0,192},{64,0},{128,64},{192,128},{1,193},{65,1},{129,65},{193,129... | collective-permute-start | bytes 1597448 | tf_op jit(solution)/shard_map/ppermute | solution.py:477
  9.0 20.7 %all-to-all-start = ((bf16[32,16,256]{2,1,0:T(8,128)(2,1)}), bf16[32,16,256]{2,1,0:T(8,128)(2,1)S(1)}, u32[]{:S(2)}, u32[]{:S(2)}) async-start(bf16[32,16,256]{2,1,0:T(8,128)(2,1)} %get-tuple-element.15), calls=%async_computation | async-start | bytes 524288 | tf_op jit(solution)/shard_map/all_to_all | solution.py:488
  20.1 10.8 %collective-permute-start.3 = (bf16[130,16,128]{2,1,0:T(8,128)(2,1)S(1)}, bf16[130,16,128]{2,1,0:T(8,128)(2,1)S(1)}, u32[]{:S(2)}, u32[]{:S(2)}) collective-permute-start(bf16[130,16,128]{2,1,0:T(8,128)(2,1)S(1)} %get-tuple-element.18.refs_0_), channel_id=1, source_target_pairs={{0,32},{32,0},{1,33},{33,1},{2,34},{34,2},{3,35},{35,3},{4,36},{36... | collective-permute-start | bytes 1597448 | tf_op jit(solution)/shard_map/ppermute | solution.py:480
  21.5 9.4 %collective-permute-start.4 = (bf16[130,16,128]{2,1,0:T(8,128)(2,1)S(1)}, bf16[130,16,128]{2,1,0:T(8,128)(2,1)S(1)}, u32[]{:S(2)}, u32[]{:S(2)}) collective-permute-start(bf16[130,16,128]{2,1,0:T(8,128)(2,1)S(1)} %collective-permute-done.near_ref.refs_2_), channel_id=1, source_target_pairs={{0,32},{32,0},{1,33},{33,1},{2,34},{34,2},{3,35},{35,3},{4,36},{36... | collective-permute-start | bytes 1597448 | tf_op jit(solution)/shard_map/ppermute | solution.py:480
  22.0 8.9 %collective-permute-start.5 = (bf16[130,16,128]{2,1,0:T(8,128)(2,1)S(1)}, bf16[130,16,128]{2,1,0:T(8,128)(2,1)S(1)}, u32[]{:S(2)}, u32[]{:S(2)}) collective-permute-start(bf16[130,16,128]{2,1,0:T(8,128)(2,1)S(1)} %collective-permute-done.1.far_ref.refs_4_), channel_id=1, source_target_pairs={{0,32},{32,0},{1,33},{33,1},{2,34},{34,2},{3,35},{35,3},{4,36},{36... | collective-permute-start | bytes 1597448 | tf_op jit(solution)/shard_map/ppermute | solution.py:480
  22.9 12.5 %collective-permute-start.2 = (bf16[130,16,128]{2,1,0:T(8,128)(2,1)}, bf16[130,16,128]{2,1,0:T(8,128)(2,1)}, u32[]{:S(2)}, u32[]{:S(2)}) collective-permute-start(bf16[130,16,128]{2,1,0:T(8,128)(2,1)} %onward.1), channel_id=1, source_target_pairs={{0,64},{64,128},{128,192},{192,0},{32,224},{96,32},{160,96},{224,1... | collective-permute-start | bytes 1597448 | tf_op jit(solution)/shard_map/ppermute | solution.py:483
  35.4 5.5 %collective-permute-start.6 = (bf16[130,16,128]{2,1,0:T(8,128)(2,1)}, bf16[130,16,128]{2,1,0:T(8,128)(2,1)S(1)}, u32[]{:S(2)}, u32[]{:S(2)}) collective-permute-start(bf16[130,16,128]{2,1,0:T(8,128)(2,1)} %collective-permute-done.2.block_ref), channel_id=1, source_target_pairs={{0,32},{32,0},{1,33},{33,1},{2,34},{34,2},{3,35},{35,3},{4,36},{36... | collective-permute-start | bytes 1597448 | tf_op jit(solution)/shard_map/ppermute | solution.py:480

commit v5 on v4

--- a/solution.py
+++ b/solution.py
@@ -347,7 +347,7 @@
         sum_ref[tile] = jnp.concatenate(total, axis=1)
         return carry
 
-    lax.fori_loop(0, PLANE, step, 0, unroll=8)
+    lax.fori_loop(0, PLANE, step, 0, unroll=16 if last else 8)
     if last:
         part_ref[...] = sum_ref[...].reshape(PLANE * ROWS, PIX).astype(jnp.bfloat16)
 

time: 87.4 us -> 87.3 us (level)
  no operation moved by 1% of the time
where the time goes in v5:
time: 87.3 us; the launch traced here: 86.9 us
  blocking collectives  39.9 us (46%)
  starting transfers between devices  23.1 us (26%)
  Pallas kernels  15.7 us (18%)
  waiting for transfers between devices  4.72 us (5%)
  local copies, waits for them, and re-layouts  2.06 us (2%)
    all_to_all x1, blocking collectives, body(): lax.all_to_all(parts.reshape(PLANE, ROWS, PIX), ('x', 'z'), 0, 0, tiled=T...  15.1 us
    all_to_all x1, blocking collectives, body(): images = lax.all_to_all(copies, ('x', 'z'), 0, 0, tiled=True)  13.8 us
    all_to_all x1, blocking collectives, body(): grads = lax.all_to_all(grads, ('y', 'core'), 0, 0, tiled=True)  11 us
    all_to_all x1, starting transfers between devices, body(): known = lax.all_to_all(known, ('x', 'z'), 0, 0, tiled=True)  11 us
    pallas_call x2, Pallas kernels, image_parts(): pl.pallas_call(functools.partial(image_kernel, first, count, parts, last)...  7.11 us
    ppermute x4, starting transfers between devices, pair(): lax.ppermute(x, 'core', [(0, 1), (1, 0)])  5.66 us
    all_to_all x1, waiting for transfers between devices, body(): known = lax.all_to_all(known, ('x', 'z'), 0, 0, tiled=True)  4.03 us
    ppermute x2, starting transfers between devices, back_by(): return lax.ppermute(x, 'y', [(at, (at + steps) % 4) for at in range(4)])  3.74 us
  transfers between devices with their start and end apart: 8, of which 2 were waited for; matrix products, arithmetic and copies ran while one was open for 0% of the time, Pallas kernels for 9%

profile of v5, /device:TPU:1, one launch (start us, length us, event | category | flops | bytes accessed | tf_op | source)
XLA Modules:
  0.0 86.9 jit_solution(8165572627176551409)
XLA Ops:
  0.6 0.0 copy-start.5
  0.6 0.0 copy-start.1
  0.7 0.0 copy-start.2
  0.7 0.0 copy-start
  0.7 0.0 copy-start.3
  0.7 0.0 copy-start.4
  0.7 1.4 %reshape.16 = bf16[2,4,2,64,256]{4,3,2,1,0:T(8,128)(2,1)S(1)} reshape(bf16[2,4,2,16384]{3,2,1,0:T(2,128)(2,1)} %param.7) | data formatting | bytes 1048576 | tf_op jit(solution)/shard_map/reshape | solution.py:466
  2.1 0.4 copy.11
  2.5 0.1 reshape.17.raw_ref
  2.6 0.0 copy-done.5
  2.7 0.0 copy-done.1
  2.7 0.0 copy-done.2
  2.7 0.0 copy-done
  2.7 0.0 copy-done.3
  2.7 0.0 copy-done.4
  2.7 2.6 %compress.1 = (bf16[130,16,128]{2,1,0:T(8,128)(2,1)S(1)}, bf16[32,16,256]{2,1,0:T(8,128)(2,1)}) custom-call(bf16[1024,256]{1,0:T(8,128)(2,1)S(1)} %reshape.17.raw_ref, f32[2,1280]{1,0:T(2,128)S(1)} %pad.4.taps_ref, f32[2]{0:T(128)S(1)} %copy-done.4, s32[2,256]{1,0:T(2,128)S(1)} %bitcast.23, s32[2,256]{1,0:T(2,128)S(1)} %bitcast.24, s32[8,256]{1,0:T(8,128)S(1)} %bitcast.22, ...), custom_call_target="tpu_custom_call" | custom-call | tf_op jit(solution)/shard_map/compress/pallas_call | solution.py:127
  5.3 2.2 %collective-permute-start = (bf16[130,16,128]{2,1,0:T(8,128)(2,1)S(1)}, bf16[130,16,128]{2,1,0:T(8,128)(2,1)S(1)}, u32[]{:S(2)}, u32[]{:S(2)}) collective-permute-start(bf16[130,16,128]{2,1,0:T(8,128)(2,1)S(1)} %get-tuple-element.18.refs_0_), channel_id=1, source_target_pairs={{0,64},{64,128},{128,192},{192,0},{1,65},{65,129},{129,193},{193,1... | collective-permute-start | bytes 1597448 | tf_op jit(solution)/shard_map/ppermute | solution.py:477
  7.5 1.5 %collective-permute-start.1 = (bf16[130,16,128]{2,1,0:T(8,128)(2,1)S(1)}, bf16[130,16,128]{2,1,0:T(8,128)(2,1)S(1)}, u32[]{:S(2)}, u32[]{:S(2)}) collective-permute-start(bf16[130,16,128]{2,1,0:T(8,128)(2,1)S(1)} %get-tuple-element.18.refs_0_), channel_id=1, source_target_pairs={{0,192},{64,0},{128,64},{192,128},{1,193},{65,1},{129,65},{193,129... | collective-permute-start | bytes 1597448 | tf_op jit(solution)/shard_map/ppermute | solution.py:477
  9.0 11.0 %all-to-all-start = ((bf16[32,16,256]{2,1,0:T(8,128)(2,1)}), bf16[32,16,256]{2,1,0:T(8,128)(2,1)S(1)}, u32[]{:S(2)}, u32[]{:S(2)}) async-start(bf16[32,16,256]{2,1,0:T(8,128)(2,1)} %get-tuple-element.15), calls=%async_computation | async-start | bytes 524288 | tf_op jit(solution)/shard_map/all_to_all | solution.py:488
  20.1 1.5 %collective-permute-start.3 = (bf16[130,16,128]{2,1,0:T(8,128)(2,1)S(1)}, bf16[130,16,128]{2,1,0:T(8,128)(2,1)S(1)}, u32[]{:S(2)}, u32[]{:S(2)}) collective-permute-start(bf16[130,16,128]{2,1,0:T(8,128)(2,1)S(1)} %get-tuple-element.18.refs_0_), channel_id=1, source_target_pairs={{0,32},{32,0},{1,33},{33,1},{2,34},{34,2},{3,35},{35,3},{4,36},{36... | collective-permute-start | bytes 1597448 | tf_op jit(solution)/shard_map/ppermute | solution.py:480
  21.5 0.0 collective-permute-done.near_ref.refs_2_
  21.5 0.5 collective-permute-start.4
  22.0 0.0 collective-permute-done.1.far_ref.refs_4_
  22.0 0.0 collective-permute-start.5
  22.0 0.8 onward.1
  22.9 2.7 %collective-permute-start.2 = (bf16[130,16,128]{2,1,0:T(8,128)(2,1)}, bf16[130,16,128]{2,1,0:T(8,128)(2,1)}, u32[]{:S(2)}, u32[]{:S(2)}) collective-permute-start(bf16[130,16,128]{2,1,0:T(8,128)(2,1)} %onward.1), channel_id=1, source_target_pairs={{0,64},{64,128},{128,192},{192,0},{32,224},{96,32},{160,96},{224,1... | collective-permute-start | bytes 1597448 | tf_op jit(solution)/shard_map/ppermute | solution.py:483
  25.6 0.1 stack.35.group_ref
  25.7 4.0 %all-to-all-done.known_ref = bf16[32,16,256]{2,1,0:T(8,128)(2,1)S(1)} async-done(((bf16[32,16,256]{2,1,0:T(8,128)(2,1)}), bf16[32,16,256]{2,1,0:T(8,128)(2,1)S(1)}, u32[]{:S(2)}, u32[]{:S(2)}) %all-to-all-start) | async-done | bytes 262176 | tf_op jit(solution)/shard_map/all_to_all | solution.py:488
  29.7 1.1 %phases.1 = (s32[8,32,256]{2,1,0:T(8,128)S(1)}, f32[8,2,32,256]{3,2,1,0:T(8,128)S(1)}) custom-call(s32[8]{0:T(128)S(1)} %stack.35.group_ref, f32[8]{0:T(128)S(1)} %convert_multiply_fusion.rate_ref, bf16[32,16,256]{2,1,0:T(8,128)(2,1)S(1)} %all-to-all-done.known_ref), custom_call_target="tpu_custom_call" | custom-call | flops 1200000000 | bytes 1000000 | tf_op jit(solution)/shard_map/phases/pallas_call | solution.py:267
  30.9 0.0 collective-permute-done.3.refs_1_
  30.9 0.0 collective-permute-done.4.refs_3_
  30.9 0.0 collective-permute-done.5.refs_5_
  30.9 4.5 %image.2 = (f32[32,8,256]{2,1,0:T(8,128)S(1)}, bf16[32,6,16,256]{3,2,1,0:T(8,128)(2,1)S(1)}, s32[32,128]{1,0:T(8,128)S(1)}) custom-call(s32[1]{0:T(128)} %bitcast.group_ref, s32[8,32,256]{2,1,0:T(8,128)S(1)} %get-tuple-element.16.bins_ref, f32[8,2,32,256]{3,2,1,0:T(8,128)S(1)} %get-tuple-element.17.phase_ref, ...), custom_call_target="tpu_custom_call" | custom-call | flops 600000000 | bytes 1000000 | tf_op jit(solution)/shard_map/image/pallas_call | solution.py:360
  35.4 0.0 collective-permute-done.2.block_ref
  35.4 3.7 %collective-permute-start.6 = (bf16[130,16,128]{2,1,0:T(8,128)(2,1)}, bf16[130,16,128]{2,1,0:T(8,128)(2,1)S(1)}, u32[]{:S(2)}, u32[]{:S(2)}) collective-permute-start(bf16[130,16,128]{2,1,0:T(8,128)(2,1)} %collective-permute-done.2.block_ref), channel_id=1, source_target_pairs={{0,32},{32,0},{1,33},{33,1},{2,34},{34,2},{3,35},{35,3},{4,36},{36... | collective-permute-start | bytes 1597448 | tf_op jit(solution)/shard_map/ppermute | solution.py:480
  39.1 1.1 %fetch.1.refs_0_ = bf16[130,16,128]{2,1,0:T(8,128)(2,1)S(1)} custom-call(bf16[130,16,128]{2,1,0:T(8,128)(2,1)} %collective-permute-done.2.block_ref), custom_call_target="tpu_custom_call" | custom-call | flops 1200000000 | bytes 4000000 | tf_op jit(solution)/shard_map/fetch/pallas_call | solution.py:176
  40.1 0.7 collective-permute-done.6.refs_1_
  40.8 2.7 %image.3 = (bf16[256,256]{1,0:T(8,128)(2,1)S(1)}, bf16[32,2,16,256]{3,2,1,0:T(8,128)(2,1)S(1)}, s32[32,128]{1,0:T(8,128)S(1)}) custom-call(s32[1]{0:T(128)} %bitcast.group_ref, s32[8,32,256]{2,1,0:T(8,128)S(1)} %get-tuple-element.16.bins_ref, f32[8,2,32,256]{3,2,1,0:T(8,128)S(1)} %get-tuple-element.17.phase_ref, bf16[130,16,128]{2,1,0:T(8,128)(2,1)S(1)} %fetch.1.refs_0_, ...), custom_call_target="tpu_custom_call" | custom-call | flops 200000000 | bytes 1000000 | tf_op jit(solution)/shard_map/image/pallas_call | solution.py:360
  43.5 15.1 %all_to_all.20.parts_ref = bf16[32,8,256]{2,1,0:T(8,128)(2,1)S(1)} all-to-all(bf16[32,8,256]{2,1,0:T(8,128)(2,1)S(1)} %bitcast.21), channel_id=1, replica_groups=mesh['y'=4,'core'=2,'x'=4,'z'=8] {'x','z'}, dimensions={0} | all-to-all | bytes 262144 | tf_op jit(solution)/shard_map/all_to_all | solution.py:495
  58.5 0.7 total.1
  59.2 13.8 %all_to_all.21.image_ref = f32[32,8,256]{2,1,0:T(8,128)S(1)} all-to-all(f32[32,8,256]{2,1,0:T(8,128)S(1)} %get-tuple-element.25), channel_id=1, replica_groups=mesh['y'=4,'core'=2,'x'=4,'z'=8] {'x','z'}, dimensions={0} | all-to-all | bytes 524288 | tf_op jit(solution)/shard_map/all_to_all | solution.py:497
  73.0 2.4 %grad.1 = f32[8,1,128]{2,1,0:T(1,128)S(1)} custom-call(s32[8]{0:T(128)S(1)} %stack.35.group_ref, s32[32,128]{1,0:T(8,128)S(1)} %get-tuple-element.23.whole_a, s32[32,128]{1,0:T(8,128)S(1)} %get-tuple-element.24.whole_b, f32[32,8,256]{2,1,0:T(8,128)S(1)} %all_to_all.21.image_ref, bf16[32,6,16,256]{3,2,1,0:T(8,128)(2,1)S(1)} %get-tuple-element.26.kept_a, ...), custom_call_target="tpu_custom_call" | custom-call | tf_op jit(solution)/shard_map/grad/pallas_call | solution.py:449
  75.4 11.0 %all_to_all.22 = f32[8,1,128]{2,1,0:T(1,128)S(1)} all-to-all(f32[8,1,128]{2,1,0:T(1,128)S(1)} %grad.1), channel_id=1, replica_groups=mesh['y'=4,'core'=2,'x'=4,'z'=8] {'y','core'}, dimensions={0} | all-to-all | bytes 8192 | tf_op jit(solution)/shard_map/all_to_all | solution.py:499
  86.4 0.5 slice_reduce_fusion
  (2 shorter events, 0.0 us)
Async XLA Ops:
  0.6 2.0 %copy-start.5 = (f32[2,1024]{1,0:T(2,128)S(1)}, f32[2,1024]{1,0:T(2,128)}, u32[]{:S(2)}) copy-start(f32[2,1024]{1,0:T(2,128)} %param.8) | copy-start | bytes 24580
  0.6 2.0 %copy-start.1 = (s32[1,256,2]{1,2,0:T(2,128)S(1)}, s32[1,256,2]{1,2,0:T(2,128)}, u32[]{:S(2)}) copy-start(s32[1,256,2]{1,2,0:T(2,128)} %param.10) | copy-start | bytes 6148
  0.7 2.0 %copy-start.2 = (s32[1,256,2]{1,2,0:T(2,128)S(1)}, s32[1,256,2]{1,2,0:T(2,128)}, u32[]{:S(2)}) copy-start(s32[1,256,2]{1,2,0:T(2,128)} %param.11) | copy-start | bytes 6148
  0.7 2.0 %copy-start = (s32[1,8,256]{2,1,0:T(8,128)S(1)}, s32[1,8,256]{2,1,0:T(8,128)}, u32[]{:S(2)}) copy-start(s32[1,8,256]{2,1,0:T(8,128)} %param.12) | copy-start | bytes 24580
  0.7 2.0 %copy-start.3 = (f32[1,256]{1,0:T(1,128)S(1)}, f32[1,256]{1,0:T(1,128)}, u32[]{:S(2)}) copy-start(f32[1,256]{1,0:T(1,128)} %cross_hbm.1) | copy-start | bytes 3076
  0.7 2.0 %copy-start.4 = (f32[2]{0:T(128)S(1)}, f32[2]{0:T(128)}, u32[]{:S(2)}) copy-start(f32[2]{0:T(128)} %error_hbm.1) | copy-start | bytes 28
  5.3 16.2 %collective-permute-start = (bf16[130,16,128]{2,1,0:T(8,128)(2,1)S(1)}, bf16[130,16,128]{2,1,0:T(8,128)(2,1)S(1)}, u32[]{:S(2)}, u32[]{:S(2)}) collective-permute-start(bf16[130,16,128]{2,1,0:T(8,128)(2,1)S(1)} %get-tuple-element.18.refs_0_), channel_id=1, source_target_pairs={{0,64},{64,128},{128,192},{192,0},{1,65},{65,129},{129,193},{193,1... | collective-permute-start | bytes 1597448 | tf_op jit(solution)/shard_map/ppermute | solution.py:477
  7.5 14.5 %collective-permute-start.1 = (bf16[130,16,128]{2,1,0:T(8,128)(2,1)S(1)}, bf16[130,16,128]{2,1,0:T(8,128)(2,1)S(1)}, u32[]{:S(2)}, u32[]{:S(2)}) collective-permute-start(bf16[130,16,128]{2,1,0:T(8,128)(2,1)S(1)} %get-tuple-element.18.refs_0_), channel_id=1, source_target_pairs={{0,192},{64,0},{128,64},{192,128},{1,193},{65,1},{129,65},{193,129... | collective-permute-start | bytes 1597448 | tf_op jit(solution)/shard_map/ppermute | solution.py:477
  9.0 20.7 %all-to-all-start = ((bf16[32,16,256]{2,1,0:T(8,128)(2,1)}), bf16[32,16,256]{2,1,0:T(8,128)(2,1)S(1)}, u32[]{:S(2)}, u32[]{:S(2)}) async-start(bf16[32,16,256]{2,1,0:T(8,128)(2,1)} %get-tuple-element.15), calls=%async_computation | async-start | bytes 524288 | tf_op jit(solution)/shard_map/all_to_all | solution.py:488
  20.1 10.8 %collective-permute-start.3 = (bf16[130,16,128]{2,1,0:T(8,128)(2,1)S(1)}, bf16[130,16,128]{2,1,0:T(8,128)(2,1)S(1)}, u32[]{:S(2)}, u32[]{:S(2)}) collective-permute-start(bf16[130,16,128]{2,1,0:T(8,128)(2,1)S(1)} %get-tuple-element.18.refs_0_), channel_id=1, source_target_pairs={{0,32},{32,0},{1,33},{33,1},{2,34},{34,2},{3,35},{35,3},{4,36},{36... | collective-permute-start | bytes 1597448 | tf_op jit(solution)/shard_map/ppermute | solution.py:480
  21.5 9.4 %collective-permute-start.4 = (bf16[130,16,128]{2,1,0:T(8,128)(2,1)S(1)}, bf16[130,16,128]{2,1,0:T(8,128)(2,1)S(1)}, u32[]{:S(2)}, u32[]{:S(2)}) collective-permute-start(bf16[130,16,128]{2,1,0:T(8,128)(2,1)S(1)} %collective-permute-done.near_ref.refs_2_), channel_id=1, source_target_pairs={{0,32},{32,0},{1,33},{33,1},{2,34},{34,2},{3,35},{35,3},{4,36},{36... | collective-permute-start | bytes 1597448 | tf_op jit(solution)/shard_map/ppermute | solution.py:480
  22.0 8.9 %collective-permute-start.5 = (bf16[130,16,128]{2,1,0:T(8,128)(2,1)S(1)}, bf16[130,16,128]{2,1,0:T(8,128)(2,1)S(1)}, u32[]{:S(2)}, u32[]{:S(2)}) collective-permute-start(bf16[130,16,128]{2,1,0:T(8,128)(2,1)S(1)} %collective-permute-done.1.far_ref.refs_4_), channel_id=1, source_target_pairs={{0,32},{32,0},{1,33},{33,1},{2,34},{34,2},{3,35},{35,3},{4,36},{36... | collective-permute-start | bytes 1597448 | tf_op jit(solution)/shard_map/ppermute | solution.py:480
  22.9 12.5 %collective-permute-start.2 = (bf16[130,16,128]{2,1,0:T(8,128)(2,1)}, bf16[130,16,128]{2,1,0:T(8,128)(2,1)}, u32[]{:S(2)}, u32[]{:S(2)}) collective-permute-start(bf16[130,16,128]{2,1,0:T(8,128)(2,1)} %onward.1), channel_id=1, source_target_pairs={{0,64},{64,128},{128,192},{192,0},{32,224},{96,32},{160,96},{224,1... | collective-permute-start | bytes 1597448 | tf_op jit(solution)/shard_map/ppermute | solution.py:483
  35.4 5.5 %collective-permute-start.6 = (bf16[130,16,128]{2,1,0:T(8,128)(2,1)}, bf16[130,16,128]{2,1,0:T(8,128)(2,1)S(1)}, u32[]{:S(2)}, u32[]{:S(2)}) collective-permute-start(bf16[130,16,128]{2,1,0:T(8,128)(2,1)} %collective-permute-done.2.block_ref), channel_id=1, source_target_pairs={{0,32},{32,0},{1,33},{33,1},{2,34},{34,2},{3,35},{35,3},{4,36},{36... | collective-permute-start | bytes 1597448 | tf_op jit(solution)/shard_map/ppermute | solution.py:480
